TPU v7x, 32 devices: a whole 2x2x4 slice. The times are simulated.
32 devices in a mesh: parts: 2 (over x), req: 2 (over core), tp: 8 (over z, y).
Axes of the slice: x: 2, y: 2, z: 4, core: 2. Of those that a mesh axis runs over, the one named last changes fastest.
Arguments:
- input_hidden_rows: bfloat16 [64, 8192], P(('parts', 'req')), parts along dimension 0, may hold values from -6 to 6
- input_norm_scale: bfloat16 [8192], replicated, may hold values from 0.099609375 to 1.8984375
- query_weight: bfloat16 [8192, 4096], P(None, 'tp'), may hold values from -0.0625 to 0.0625
- key_value_weight: bfloat16 [8192, 1024], P(None, 'tp'), may hold values from -0.0625 to 0.0625
- output_weight: bfloat16 [4096, 8192], P('tp'), may hold values from -0.125 to 0.125
- cache: bfloat16 [64, 512, 1024], P(('parts', 'req', 'tp')), parts along dimension 0, may hold values from -2000 to 2000
- lengths: int32 [64], P(('parts', 'req', 'tp')), parts along dimension 0, may hold values from 2 to 512, as said below
- adapter_per_block: int32 [4], P(('parts', 'req')), parts along dimension 0, may hold values from 0 to 127
- adapter_storage_slot: int32 [128], replicated, may hold values from 0 to 127, each once
- adapter_down_projection: bfloat16 [128, 16, 4096], P('req', None, 'tp'), may hold values from -0.09375 to 0.09375
- adapter_up_projection: bfloat16 [128, 16, 8192], P('req', None, 'tp'), may hold values from -3 to 3
Outputs:
- hidden_out: bfloat16 [64, 8192], P(('parts', 'req')), parts along dimension 0
- new_pairs: bfloat16 [2, 64, 1024], P(None, ('parts', 'req', 'tp')), parts along dimension 1
There are 2 independent parts, one for each index of `parts`. A program takes and returns all parts, laid end to end along the dimension named above; an argument that names none is the same for every part. Nothing has to cross between parts.
Inputs may be any that keep to these rules, and one draw needn't show every extreme that they name: `lengths`: each row has at least two valid positions and some row of every draw has 512.
All inputs are finite; a program needn't handle non-finite values.
Results may differ from a plain program's by a relative error of at most 0.025.
The roundings to bfloat16 on the way count: a program that leaves them out, or rounds other values in their place, can miss the bound.
Values may be sent and summed in bfloat16 or wider, within the bound.
No kernel may reach another device: no remote copies, remote signals or barrier semaphores. Data moves between devices by JAX's collectives and lax.ppermute only.
A program may use at most 128 MiB of HBM per device.

v0:
```python
import math

import jax
import jax.numpy as jnp
from jax import lax
from jax.sharding import PartitionSpec as P

MODEL_WIDTH = 8192
HEAD_SIZE = 128
QUERY_HEAD_COUNT = 32
KV_HEADS = 4
BLOCK = 16
STEPS = 2


rope_base = 500000.0
norm_epsilon = 1e-05


def rotate(values_in, positions):
    half_dim = values_in.shape[-1] // 2
    frequency = rope_base ** (
        -(jnp.arange(half_dim, dtype=jnp.float32) * 2.0 / values_in.shape[-1])
    )
    angles = positions.astype(jnp.float32)[:, None, None] * frequency[None, None, :]
    cosine = jnp.cos(angles)
    sine_part = jnp.sin(angles)
    front_half = values_in[..., :half_dim]
    back_half = values_in[..., half_dim:]
    return jnp.concatenate(
        [front_half * cosine - back_half * sine_part, back_half * cosine + front_half * sine_part],
        axis=-1,
    )


def local(
    input_hidden_rows,
    input_norm_scale,
    query_weight,
    key_value_weight,
    output_weight,
    cache,
    lengths,
    adapter_per_block,
    adapter_storage_slot,
    adapter_down_projection,
    adapter_up_projection,
):
    tp_count = lax.axis_size("tp")
    rows_req = input_hidden_rows.shape[0]
    att_rows = cache.shape[0]
    context = cache.shape[1]
    half_kv = cache.shape[2] // 2
    groups = QUERY_HEAD_COUNT // KV_HEADS
    block_count = rows_req // BLOCK
    slot_in_storage = adapter_storage_slot[adapter_per_block]
    all_down, all_up = (
        lax.all_gather(adapter_down_projection, "req", axis=0, tiled=True),
        lax.all_gather(adapter_up_projection, "req", axis=0, tiled=True),
    )
    down_matrices = jnp.take(all_down, slot_in_storage, axis=0)
    up_matrices = jnp.take(all_up, slot_in_storage, axis=0)
    cache_keys = cache[:, :, :half_kv].reshape(att_rows, context, KV_HEADS, HEAD_SIZE)
    cache_values = cache[:, :, half_kv:].reshape(att_rows, context, KV_HEADS, HEAD_SIZE)
    cache_valid = jnp.arange(context, dtype=jnp.int32)[None, :] < lengths[:, None]
    share_width = MODEL_WIDTH // tp_count
    share_start = lax.axis_index("tp") * share_width
    hidden = input_hidden_rows
    fresh_keys = []
    fresh_values = []
    stored = []
    for decode_step in range(STEPS):
        wide_hidden = hidden.astype(jnp.float32)
        normed = (
            wide_hidden
            * lax.rsqrt(jnp.mean(wide_hidden * wide_hidden, axis=-1, keepdims=True) + norm_epsilon)
            * input_norm_scale.astype(jnp.float32)
        ).astype(jnp.bfloat16)
        query_heads = jnp.dot(normed, query_weight, preferred_element_type=jnp.float32).astype(
            jnp.bfloat16
        )
        fresh_pairs = jnp.dot(normed, key_value_weight, preferred_element_type=jnp.float32).astype(
            jnp.bfloat16
        )
        query_rows, pair_rows = (
            lax.all_to_all(query_heads, "tp", split_axis=0, concat_axis=1, tiled=True),
            lax.all_to_all(fresh_pairs, "tp", split_axis=0, concat_axis=1, tiled=True),
        )
        positions = lengths + decode_step
        rotated_query = rotate(
            query_rows.astype(jnp.float32).reshape(att_rows, QUERY_HEAD_COUNT, HEAD_SIZE), positions
        ).astype(jnp.bfloat16)
        key_new = rotate(
            pair_rows[:, :half_kv].astype(jnp.float32).reshape(att_rows, KV_HEADS, HEAD_SIZE),
            positions,
        ).astype(jnp.bfloat16)
        value_new = pair_rows[:, half_kv:]
        stored.append(jnp.concatenate([key_new.reshape(att_rows, half_kv), value_new], axis=1))
        fresh_keys.append(key_new)
        fresh_values.append(value_new.reshape(att_rows, KV_HEADS, HEAD_SIZE))
        key_block = jnp.concatenate([cache_keys, jnp.stack(fresh_keys, axis=1)], axis=1)
        value_block = jnp.concatenate([cache_values, jnp.stack(fresh_values, axis=1)], axis=1)
        valid_mask = jnp.concatenate(
            [cache_valid, jnp.ones((att_rows, decode_step + 1), dtype=bool)], axis=1
        )
        grouped = rotated_query.reshape(att_rows, KV_HEADS, groups, HEAD_SIZE)
        scores = jnp.einsum(
            "rkgd,rpkd->rkgp", grouped, key_block, preferred_element_type=jnp.float32
        ) / math.sqrt(HEAD_SIZE)
        scores = jnp.where(valid_mask[:, None, None, :], scores, jnp.float32(-1e30))
        row_peak = jnp.max(scores, axis=-1, keepdims=True)
        weights = jnp.where(
            valid_mask[:, None, None, :], jnp.exp(scores - row_peak), jnp.float32(0.0)
        )
        softmax_out = (weights / jnp.sum(weights, axis=-1, keepdims=True)).astype(jnp.bfloat16)
        attention = (
            jnp.einsum(
                "rkgp,rpkd->rkgd", softmax_out, value_block, preferred_element_type=jnp.float32
            )
            .astype(jnp.bfloat16)
            .reshape(att_rows, QUERY_HEAD_COUNT * HEAD_SIZE)
        )
        head_major = lax.all_to_all(attention, "tp", split_axis=1, concat_axis=0, tiled=True)
        blocked = head_major.reshape(block_count, BLOCK, head_major.shape[1])
        low_terms = jnp.einsum(
            "bte,bre->btr", blocked, down_matrices, preferred_element_type=jnp.float32
        )
        low_rank = lax.psum(low_terms, "tp").astype(jnp.bfloat16)
        adapted = jnp.einsum(
            "btr,brd->btd", low_rank, up_matrices, preferred_element_type=jnp.float32
        ).reshape(rows_req, share_width)
        projected = jnp.dot(head_major, output_weight, preferred_element_type=jnp.float32)
        own_cols = lax.dynamic_slice_in_dim(projected, share_start, share_width, 1) + adapted
        projected = lax.dynamic_update_slice_in_dim(projected, own_cols, share_start, 1)
        summed = lax.psum(projected, "tp")
        hidden = (wide_hidden + summed).astype(jnp.bfloat16)
    return (hidden, jnp.stack(stored, axis=0))


def solution(mesh):
    in_specs = (
        P(("parts", "req"), None),
        P(),
        P(None, "tp"),
        P(None, "tp"),
        P("tp", None),
        P(("parts", "req", "tp"), None, None),
        P(("parts", "req", "tp")),
        P(("parts", "req")),
        P(),
        P("req", None, "tp"),
        P("req", None, "tp"),
    )
    out_specs = (P(("parts", "req"), None), P(None, ("parts", "req", "tp"), None))
    return jax.shard_map(local, mesh=mesh, in_specs=in_specs, out_specs=out_specs, check_vma=False)
```

profile of v0, /device:TPU:0, one launch (start us, length us, event | category | flops | bytes accessed | tf_op | source)
XLA Modules:
  0.0 295.4 jit_solution(6130695698537433887)
XLA Ops:
  7.2 0.7 all-gather.3.cloned.1.call-update
  8.0 0.7 all-gather.5.cloned.1.call-update
  8.7 0.2 fusion.34
  8.9 1.0 convolution_convert_fusion.5
  10.0 7.3 %all-to-all-start.1 = ((bf16[8,2,128]{2,1,0:T(2,128)(2,1)}), bf16[8,2,128]{2,1,0:T(2,128)(2,1)S(1)}, u32[]{:S(2)}, u32[]{:S(2)}) async-start(bf16[8,2,128]{2,1,0:T(2,128)(2,1)} %bitcast.4), calls=%async_computation.1 | async-start | bytes 8192 | tf_op jit(solution)/shard_map/all_to_all | solution.py:87
  17.3 0.1 multiply_cosine_fusion
  17.4 3.2 %fusion.89 = (bf16[2,512,512]{2,1,0:T(8,128)(2,1)}, bf16[2,512,512]{2,1,0:T(8,128)(2,1)}) fusion(bf16[2,512,1024]{2,1,0:T(8,128)(2,1)} %param.16), kind=kLoop, calls=%fused_computation.130 | loop fusion | bytes 4194304 | tf_op jit(solution)/shard_map/slice | solution.py:63
  20.6 4.8 %convolution_convert_fusion.3 = bf16[16,512]{1,0:T(8,128)(2,1)S(1)} fusion(bf16[8192,512]{1,0:T(8,128)(2,1)} %param.13, bf16[16,8192]{1,0:T(8,128)(2,1)S(1)} %copy-done.1, f32[8192]{0:T(1024)S(1)} %convert_element_type.111, f32[16]{0:T(128)S(1)} %add_rsqrt_fusion.1), kind=kOutput, calls=%fused_computation.19 | convolution fusion | flops 134750208 | bytes 8699968 | tf_op jit(solution)/shard_map/dot_general | solution.py:79
  25.5 0.6 all_to_all.76
  26.1 1.5 copy.64
  27.6 1.3 copy.51
  28.9 1.5 copy.65
  30.4 1.3 copy.53
  31.8 6.0 %all-to-all-start = ((bf16[8,2,512]{2,1,0:T(2,128)(2,1)}), bf16[8,2,512]{2,1,0:T(2,128)(2,1)S(1)}, u32[]{:S(2)}, u32[]{:S(2)}) async-start(bf16[8,2,512]{2,1,0:T(2,128)(2,1)} %all_to_all.76), calls=%async_computation | async-start | bytes 32768 | tf_op jit(solution)/shard_map/all_to_all | solution.py:86
  37.9 6.4 %all-to-all-done = bf16[8,2,512]{2,1,0:T(2,128)(2,1)S(1)} async-done(((bf16[8,2,512]{2,1,0:T(2,128)(2,1)}), bf16[8,2,512]{2,1,0:T(2,128)(2,1)S(1)}, u32[]{:S(2)}, u32[]{:S(2)}) %all-to-all-start) | async-done | bytes 16416 | tf_op jit(solution)/shard_map/all_to_all | solution.py:86
  44.4 0.1 fusion.52
  44.5 2.4 fusion.90
  46.9 1.2 convolution_convert_fusion.2
  48.2 0.6 copy.55
  48.8 3.3 %all-to-all-start.2 = ((bf16[2,8,512]{2,0,1:T(2,128)(2,1)}), bf16[2,8,512]{2,0,1:T(2,128)(2,1)S(1)}, u32[]{:S(2)}, u32[]{:S(2)}) async-start(bf16[2,8,512]{2,0,1:T(2,128)(2,1)} %copy.55), calls=%async_computation.2 | async-start | bytes 32768 | tf_op jit(solution)/shard_map/all_to_all | solution.py:123
  52.9 0.6 dynamic-slice.8
  55.4 3.3 %all-to-all-done.2 = bf16[2,8,512]{2,0,1:T(2,128)(2,1)S(1)} async-done(((bf16[2,8,512]{2,0,1:T(2,128)(2,1)}), bf16[2,8,512]{2,0,1:T(2,128)(2,1)S(1)}, u32[]{:S(2)}, u32[]{:S(2)}) %all-to-all-start.2) | async-done | bytes 16416 | tf_op jit(solution)/shard_map/all_to_all | solution.py:123
  58.7 4.6 %fusion.98 = f32[16,8192]{1,0:T(8,128)S(1)} fusion(bf16[16,512]{1,0:T(8,128)(2,1)S(1)} %all_to_all.85, bf16[512,8192]{1,0:T(8,128)(2,1)} %param.15), kind=kOutput, calls=%fused_computation.133 | convolution fusion | flops 134217728 | bytes 8929280 | tf_op jit(solution)/shard_map/dot_general | solution.py:132
  63.3 0.8 convolution_bitcast_fusion.1
  64.1 18.7 %psum.28 = bf16[1,16,16]{2,1,0:T(8,128)(2,1)S(1)} all-reduce(f32[1,16,16]{2,1,0:T(8,128)S(1)} %convolution_bitcast_fusion.1), channel_id=1, replica_groups=mesh['parts'=2,'req'=2,'tp'=8] {'tp'}, use_global_device_ids=true, to_apply=%region_3.4 | all-reduce | flops 256 | bytes 1536 | tf_op jit(solution)/shard_map/psum | solution.py:128
  82.9 0.9 fusion.11
  83.8 0.8 copy-done.2
  84.7 69.8 %all-reduce.5.cloned.1.call-done = f32[16,8192]{1,0:T(8,128)} async-done(((f32[16,8192]{1,0:T(8,128)}), f32[16,8192]{1,0:T(8,128)}) %all-reduce.5.cloned.1.call-update) | async-done | bytes 524304 | tf_op jit(solution)/shard_map/psum | solution.py:135
  154.5 1.2 fusion.38
  155.7 1.1 convolution_convert_fusion.4
  156.8 3.9 %all-to-all-start.4 = ((bf16[8,2,128]{2,1,0:T(2,128)(2,1)}), bf16[8,2,128]{2,1,0:T(2,128)(2,1)S(1)}, u32[]{:S(2)}, u32[]{:S(2)}) async-start(bf16[8,2,128]{2,1,0:T(2,128)(2,1)} %bitcast.22), calls=%async_computation.4 | async-start | bytes 8192 | tf_op jit(solution)/shard_map/all_to_all | solution.py:87
  160.7 4.6 %convolution_convert_fusion.1 = bf16[16,512]{1,0:T(8,128)(2,1)S(1)} fusion(bf16[8192,512]{1,0:T(8,128)(2,1)} %param.13, bf16[16,8192]{1,0:T(8,128)(2,1)S(1)} %get-tuple-element.36, f32[16]{0:T(128)S(1)} %add_rsqrt_fusion, f32[8192]{0:T(1024)S(1)} %convert_element_type.111), kind=kOutput, calls=%fused_computation.17 | convolution fusion | flops 134750208 | bytes 8699968 | tf_op jit(solution)/shard_map/dot_general | solution.py:79
  165.3 0.6 all_to_all.86
  165.9 1.2 all-to-all-done.4
  167.0 4.8 %all-to-all-start.3 = ((bf16[8,2,512]{2,1,0:T(2,128)(2,1)}), bf16[8,2,512]{2,1,0:T(2,128)(2,1)S(1)}, u32[]{:S(2)}, u32[]{:S(2)}) async-start(bf16[8,2,512]{2,1,0:T(2,128)(2,1)} %all_to_all.86), calls=%async_computation.3 | async-start | bytes 32768 | tf_op jit(solution)/shard_map/all_to_all | solution.py:86
  172.1 6.4 %all-to-all-done.3 = bf16[8,2,512]{2,1,0:T(2,128)(2,1)S(1)} async-done(((bf16[8,2,512]{2,1,0:T(2,128)(2,1)}), bf16[8,2,512]{2,1,0:T(2,128)(2,1)S(1)}, u32[]{:S(2)}, u32[]{:S(2)}) %all-to-all-start.3) | async-done | bytes 16416 | tf_op jit(solution)/shard_map/all_to_all | solution.py:86
  178.5 0.1 fusion.54
  178.6 2.5 fusion.93
  181.1 1.2 convolution_convert_fusion
  182.4 8.9 %all_to_all.102 = bf16[2,8,512]{2,0,1:T(2,128)(2,1)S(1)} all-to-all(bf16[2,8,512]{2,0,1:T(2,128)(2,1)S(1)} %copy.63), channel_id=1, replica_groups=mesh['parts'=2,'req'=2,'tp'=8] {'tp'}, dimensions={1} | all-to-all | bytes 32768 | tf_op jit(solution)/shard_map/all_to_all | solution.py:123
  191.4 4.6 %fusion.99 = f32[16,8192]{1,0:T(8,128)S(1)} fusion(bf16[16,512]{1,0:T(8,128)(2,1)S(1)} %all_to_all.95, bf16[512,8192]{1,0:T(8,128)(2,1)} %param.15), kind=kOutput, calls=%fused_computation.134 | convolution fusion | flops 134217728 | bytes 8929280 | tf_op jit(solution)/shard_map/dot_general | solution.py:132
  196.0 0.8 convolution_bitcast_fusion
  196.8 18.0 %psum.30 = bf16[1,16,16]{2,1,0:T(8,128)(2,1)S(1)} all-reduce(f32[1,16,16]{2,1,0:T(8,128)S(1)} %convolution_bitcast_fusion), channel_id=1, replica_groups=mesh['parts'=2,'req'=2,'tp'=8] {'tp'}, use_global_device_ids=true, to_apply=%region_8.9 | all-reduce | flops 256 | bytes 1536 | tf_op jit(solution)/shard_map/psum | solution.py:128
  214.8 0.9 fusion.10
  215.7 0.8 copy-done.3
  216.7 0.6 pad_maximum_fusion.1
  217.3 69.8 %all-reduce.7.cloned.1.call-done = f32[16,8192]{1,0:T(8,128)} async-done(((f32[16,8192]{1,0:T(8,128)}), f32[16,8192]{1,0:T(8,128)}) %all-reduce.7.cloned.1.call-update) | async-done | bytes 524304 | tf_op jit(solution)/shard_map/psum | solution.py:135
  287.1 1.8 fusion.41
  (62 shorter events, 1.0 us)
Async XLA Ops:
  7.2 1.8 copy-start
  7.2 1.5 copy-start.1
  7.2 1.7 copy-start.6
  7.2 56.1 %all-gather.3.cloned.1.call-start = ((), (), s32[]{:S(2)}) async-start(), calls=%async_computation.6 | async-start | bytes 3145728 | tf_op jit(solution)/shard_map/all_gather | solution.py:58
  7.9 9.3 %copy-start.7 = (s32[2]{0:T(128)S(1)}, s32[2]{0:T(128)}, u32[]{:S(2)}) copy-start(s32[2]{0:T(128)} %param.17) | copy-start | bytes 28
  7.9 75.0 %all-gather.5.cloned.1.call-start = ((), (), s32[]{:S(2)}) async-start(), calls=%async_computation.7 | async-start | bytes 6291456 | tf_op jit(solution)/shard_map/all_gather | solution.py:59
  10.0 21.8 %all-to-all-start.1 = ((bf16[8,2,128]{2,1,0:T(2,128)(2,1)}), bf16[8,2,128]{2,1,0:T(2,128)(2,1)S(1)}, u32[]{:S(2)}, u32[]{:S(2)}) async-start(bf16[8,2,128]{2,1,0:T(2,128)(2,1)} %bitcast.4), calls=%async_computation.1 | async-start | bytes 8192 | tf_op jit(solution)/shard_map/all_to_all | solution.py:87
  31.7 15.2 %copy-start.4 = (bf16[2,512,4,128]{3,1,2,0:T(8,128)(2,1)S(1)}, bf16[2,512,4,128]{3,1,2,0:T(8,128)(2,1)}, u32[]{:S(2)}) copy-start(bf16[2,512,4,128]{3,1,2,0:T(8,128)(2,1)} %copy.53) | copy-start | bytes 3145732
  31.8 12.6 %all-to-all-start = ((bf16[8,2,512]{2,1,0:T(2,128)(2,1)}), bf16[8,2,512]{2,1,0:T(2,128)(2,1)S(1)}, u32[]{:S(2)}, u32[]{:S(2)}) async-start(bf16[8,2,512]{2,1,0:T(2,128)(2,1)} %all_to_all.76), calls=%async_computation | async-start | bytes 32768 | tf_op jit(solution)/shard_map/all_to_all | solution.py:86
  44.5 8.4 %copy-start.8 = (s32[128]{0:T(128)S(1)}, s32[128]{0:T(128)}, u32[]{:S(2)}) copy-start(s32[128]{0:T(128)} %param.19) | copy-start | bytes 1540
  48.8 9.9 %all-to-all-start.2 = ((bf16[2,8,512]{2,0,1:T(2,128)(2,1)}), bf16[2,8,512]{2,0,1:T(2,128)(2,1)S(1)}, u32[]{:S(2)}, u32[]{:S(2)}) async-start(bf16[2,8,512]{2,0,1:T(2,128)(2,1)} %copy.55), calls=%async_computation.2 | async-start | bytes 32768 | tf_op jit(solution)/shard_map/all_to_all | solution.py:123
  52.2 102.3 %all-reduce.5.cloned.1.call-start = ((), (), s32[]{:S(2)}) async-start(), calls=%async_computation.8 | async-start | bytes 1048576 | tf_op jit(solution)/shard_map/psum | solution.py:135
  83.8 0.8 copy-start.2
  156.8 10.3 %all-to-all-start.4 = ((bf16[8,2,128]{2,1,0:T(2,128)(2,1)}), bf16[8,2,128]{2,1,0:T(2,128)(2,1)S(1)}, u32[]{:S(2)}, u32[]{:S(2)}) async-start(bf16[8,2,128]{2,1,0:T(2,128)(2,1)} %bitcast.22), calls=%async_computation.4 | async-start | bytes 8192 | tf_op jit(solution)/shard_map/all_to_all | solution.py:87
  167.0 11.4 %all-to-all-start.3 = ((bf16[8,2,512]{2,1,0:T(2,128)(2,1)}), bf16[8,2,512]{2,1,0:T(2,128)(2,1)S(1)}, u32[]{:S(2)}, u32[]{:S(2)}) async-start(bf16[8,2,512]{2,1,0:T(2,128)(2,1)} %all_to_all.86), calls=%async_computation.3 | async-start | bytes 32768 | tf_op jit(solution)/shard_map/all_to_all | solution.py:86
  171.9 115.2 %all-reduce.7.cloned.1.call-start = ((), (), s32[]{:S(2)}) async-start(), calls=%async_computation.9 | async-start | bytes 1048576 | tf_op jit(solution)/shard_map/psum | solution.py:135
  178.6 2.5 copy-start.5
  215.7 0.8 copy-start.3
Sparse Core Ops, SparseCore 0:
  9.6 13.2 all-gather.2
  24.4 14.8 all-gather.4
  84.8 69.6 all-reduce.4
  216.6 70.4 all-reduce.6
where the time goes:
time: 297 us; the launch traced here: 295 us
  waiting for transfers between devices  158 us (53%)
  blocking collectives  45.6 us (15%)
  matrix products  31.5 us (11%)
  starting transfers between devices  25.5 us (9%)
  between operations  16.7 us (6%)
  local copies, waits for them, and re-layouts  13.2 us (4%)
  other arithmetic  4.58 us (2%)
    psum x2, waiting for transfers between devices, local(): summed = lax.psum(projected, 'tp')  140 us
    psum x2, blocking collectives, local(): low_rank = lax.psum(low_terms, 'tp').astype(jnp.bfloat16)  36.7 us
    all_to_all x2, waiting for transfers between devices, local(): lax.all_to_all(query_heads, 'tp', split_axis=0, concat_axis=1, tiled=True)  12.8 us
    all_to_all x2, starting transfers between devices, local(): lax.all_to_all(fresh_pairs, 'tp', split_axis=0, concat_axis=1, tiled=True)  11.2 us
    all_to_all x2, starting transfers between devices, local(): lax.all_to_all(query_heads, 'tp', split_axis=0, concat_axis=1, tiled=True)  10.9 us
    dot_general x2, matrix products, local(): jnp.dot(normed, query_weight, preferred_element_type=jnp.float32)  9.36 us
    dot_general x2, matrix products, local(): jnp.dot(head_major, output_weight, preferred_element_type=jnp.float32)  9.17 us
    all_to_all x1, blocking collectives, local(): lax.all_to_all(attention, 'tp', split_axis=1, concat_axis=0, tiled=True)  8.94 us
  transfers between devices with their start and end apart: 9, of which 6 were waited for; matrix products, arithmetic and copies ran while one was open for 11% of the time, Pallas kernels for 0%

commit v1 on v0

--- a/solution.py
+++ b/solution.py
@@ -33,6 +33,26 @@
     )
 
 
+def row_adapters(adapter_per_block, adapter_storage_slot, down, up, att_rows):
+    tp_count = lax.axis_size("tp")
+    own = lax.axis_index("req")
+    stored_here = down.shape[0]
+    rank = down.shape[1]
+    slot = adapter_storage_slot[adapter_per_block]
+    other_slot = lax.ppermute(slot, "req", [(0, 1), (1, 0)])
+
+    def piece(which):
+        at = jnp.clip(which - own * stored_here, 0, stored_here - 1)
+        return jnp.concatenate([jnp.take(down, at, axis=0), jnp.take(up, at, axis=0)], axis=2)
+
+    sent = lax.ppermute(piece(other_slot), "req", [(0, 1), (1, 0)])
+    held = jnp.where((slot // stored_here == own)[:, None, None], piece(slot), sent)
+    gathered = lax.all_gather(held, "tp", axis=0, tiled=False)
+    block = (lax.axis_index("tp") * att_rows) // BLOCK
+    mine = lax.dynamic_index_in_dim(gathered, block, axis=1, keepdims=False)
+    return mine[:, :, : down.shape[2]], mine[:, :, down.shape[2] :]
+
+
 def local(
     input_hidden_rows,
     input_norm_scale,
@@ -51,41 +71,42 @@
     att_rows = cache.shape[0]
     context = cache.shape[1]
     half_kv = cache.shape[2] // 2
+    query_width = query_weight.shape[1]
     groups = QUERY_HEAD_COUNT // KV_HEADS
-    block_count = rows_req // BLOCK
-    slot_in_storage = adapter_storage_slot[adapter_per_block]
-    all_down, all_up = (
-        lax.all_gather(adapter_down_projection, "req", axis=0, tiled=True),
-        lax.all_gather(adapter_up_projection, "req", axis=0, tiled=True),
+    down_own, up_own = row_adapters(
+        adapter_per_block, adapter_storage_slot, adapter_down_projection, adapter_up_projection, att_rows
     )
-    down_matrices = jnp.take(all_down, slot_in_storage, axis=0)
-    up_matrices = jnp.take(all_up, slot_in_storage, axis=0)
     cache_keys = cache[:, :, :half_kv].reshape(att_rows, context, KV_HEADS, HEAD_SIZE)
     cache_values = cache[:, :, half_kv:].reshape(att_rows, context, KV_HEADS, HEAD_SIZE)
     cache_valid = jnp.arange(context, dtype=jnp.int32)[None, :] < lengths[:, None]
-    share_width = MODEL_WIDTH // tp_count
-    share_start = lax.axis_index("tp") * share_width
-    hidden = input_hidden_rows
+    scale = input_norm_scale.astype(jnp.float32)
+
+    def norm(wide):
+        mean = jnp.mean(wide * wide, axis=-1, keepdims=True)
+        return (wide * lax.rsqrt(mean + norm_epsilon) * scale).astype(jnp.bfloat16)
+
+    def exchange(chunks):
+        return lax.all_to_all(chunks, "tp", split_axis=0, concat_axis=0, tiled=True)
+
+    def gather_rows(rows):
+        spread = exchange(jnp.broadcast_to(rows[None], (tp_count,) + rows.shape))
+        return spread.reshape(rows_req, rows.shape[1])
+
+    normed = norm(input_hidden_rows.astype(jnp.float32))
+    hidden = lax.dynamic_slice_in_dim(
+        input_hidden_rows, lax.axis_index("tp") * att_rows, att_rows, 0
+    )
     fresh_keys = []
     fresh_values = []
     stored = []
     for decode_step in range(STEPS):
-        wide_hidden = hidden.astype(jnp.float32)
-        normed = (
-            wide_hidden
-            * lax.rsqrt(jnp.mean(wide_hidden * wide_hidden, axis=-1, keepdims=True) + norm_epsilon)
-            * input_norm_scale.astype(jnp.float32)
-        ).astype(jnp.bfloat16)
-        query_heads = jnp.dot(normed, query_weight, preferred_element_type=jnp.float32).astype(
-            jnp.bfloat16
-        )
-        fresh_pairs = jnp.dot(normed, key_value_weight, preferred_element_type=jnp.float32).astype(
-            jnp.bfloat16
-        )
-        query_rows, pair_rows = (
-            lax.all_to_all(query_heads, "tp", split_axis=0, concat_axis=1, tiled=True),
-            lax.all_to_all(fresh_pairs, "tp", split_axis=0, concat_axis=1, tiled=True),
-        )
+        query_heads = jnp.dot(normed, query_weight, preferred_element_type=jnp.float32)
+        fresh_pairs = jnp.dot(normed, key_value_weight, preferred_element_type=jnp.float32)
+        sent = jnp.concatenate([query_heads, fresh_pairs], axis=1).astype(jnp.bfloat16)
+        arrived = exchange(sent.reshape(tp_count, att_rows, -1))
+        arrived = arrived.transpose(1, 0, 2)
+        query_rows = arrived[:, :, :query_width]
+        pair_rows = arrived[:, :, query_width:].reshape(att_rows, 2 * half_kv)
         positions = lengths + decode_step
         rotated_query = rotate(
             query_rows.astype(jnp.float32).reshape(att_rows, QUERY_HEAD_COUNT, HEAD_SIZE), positions
@@ -118,23 +139,22 @@
                 "rkgp,rpkd->rkgd", softmax_out, value_block, preferred_element_type=jnp.float32
             )
             .astype(jnp.bfloat16)
-            .reshape(att_rows, QUERY_HEAD_COUNT * HEAD_SIZE)
+            .reshape(att_rows, tp_count, query_width)
         )
-        head_major = lax.all_to_all(attention, "tp", split_axis=1, concat_axis=0, tiled=True)
-        blocked = head_major.reshape(block_count, BLOCK, head_major.shape[1])
-        low_terms = jnp.einsum(
-            "bte,bre->btr", blocked, down_matrices, preferred_element_type=jnp.float32
-        )
-        low_rank = lax.psum(low_terms, "tp").astype(jnp.bfloat16)
+        head_major = exchange(attention.transpose(1, 0, 2)).reshape(rows_req, query_width)
+        low_rank = jnp.einsum(
+            "rjk,jdk->rd", attention, down_own, preferred_element_type=jnp.float32
+        ).astype(jnp.bfloat16)
         adapted = jnp.einsum(
-            "btr,brd->btd", low_rank, up_matrices, preferred_element_type=jnp.float32
-        ).reshape(rows_req, share_width)
+            "rd,jdc->rjc", low_rank, up_own, preferred_element_type=jnp.float32
+        ).reshape(att_rows, MODEL_WIDTH)
+        base = hidden.astype(jnp.float32) + adapted
         projected = jnp.dot(head_major, output_weight, preferred_element_type=jnp.float32)
-        own_cols = lax.dynamic_slice_in_dim(projected, share_start, share_width, 1) + adapted
-        projected = lax.dynamic_update_slice_in_dim(projected, own_cols, share_start, 1)
-        summed = lax.psum(projected, "tp")
-        hidden = (wide_hidden + summed).astype(jnp.bfloat16)
-    return (hidden, jnp.stack(stored, axis=0))
+        terms = exchange(projected.reshape(tp_count, att_rows, MODEL_WIDTH))
+        hidden = (base + jnp.sum(terms, axis=0)).astype(jnp.bfloat16)
+        if decode_step < STEPS - 1:
+            normed = gather_rows(norm(hidden.astype(jnp.float32)))
+    return (gather_rows(hidden), jnp.stack(stored, axis=0))
 
 
 def solution(mesh):

time: 297 us -> 179 us (0.60)
  waiting for transfers between devices: 158 us -> 30.8 us
  between operations: 16.7 us -> 5.92 us
  blocking collectives: 45.6 us -> 54.2 us
  local copies, waits for them, and re-layouts: 13.2 us -> 20.4 us
  other arithmetic: 4.58 us -> 8.71 us
    psum x2 -> x0, waiting for transfers between devices: 140 us -> none  [local(): summed = lax.psum(projected, 'tp')]
    psum x2 -> x0, blocking collectives: 36.7 us -> none  [local(): low_rank = lax.psum(low_terms, 'tp').astype(jnp.bfloat16)]
    all_gather x0 -> x1, blocking collectives: none -> 34.7 us  [row_adapters(): gathered = lax.all_gather(held, 'tp', axis=0, tiled=False)]
    all_to_all x5 -> x6, waiting for transfers between devices: 17.3 us -> 30.8 us  [exchange(): return lax.all_to_all(chunks, 'tp', split_axis=0, concat_axis=0, tiled=True)]
    all_to_all x1 -> x2, blocking collectives: 8.94 us -> 19.6 us  [exchange(): return lax.all_to_all(chunks, 'tp', split_axis=0, concat_axis=0, tiled=True)]
    all_to_all x5 -> x6, starting transfers between devices: 25.4 us -> 28.3 us  [exchange(): return lax.all_to_all(chunks, 'tp', split_axis=0, concat_axis=0, tiled=True)]
  transfers between devices with their start and end apart: 9 -> 8, of which waited for: 6 -> 4; matrix products, arithmetic and copies ran while one was open for 11% -> 8% of each run, Pallas kernels for 0% -> 0%
where the time goes in v1:
time: 179 us; the launch traced here: 178 us
  blocking collectives  54.2 us (30%)
  waiting for transfers between devices  30.8 us (17%)
  matrix products  29.6 us (17%)
  starting transfers between devices  28.4 us (16%)
  local copies, waits for them, and re-layouts  20.4 us (11%)
  other arithmetic  8.71 us (5%)
  between operations  5.92 us (3%)
    all_gather x1, blocking collectives, row_adapters(): gathered = lax.all_gather(held, 'tp', axis=0, tiled=False)  34.7 us
    all_to_all x6, waiting for transfers between devices, exchange(): return lax.all_to_all(chunks, 'tp', split_axis=0, concat_axis=0, tiled=True)  30.8 us
    all_to_all x6, starting transfers between devices, exchange(): return lax.all_to_all(chunks, 'tp', split_axis=0, concat_axis=0, tiled=True)  28.3 us
    all_to_all x2, blocking collectives, exchange(): return lax.all_to_all(chunks, 'tp', split_axis=0, concat_axis=0, tiled=True)  19.6 us
    dot_general x2, matrix products, local(): jnp.dot(normed, query_weight, preferred_element_type=jnp.float32)  9.18 us
    dot_general x2, matrix products, local(): jnp.dot(head_major, output_weight, preferred_element_type=jnp.float32)  9.15 us
    sub x2, matrix products, local(): scores - row_peak  5.57 us
  transfers between devices with their start and end apart: 8, of which 4 were waited for; matrix products, arithmetic and copies ran while one was open for 8% of the time, Pallas kernels for 0%

profile of v1, /device:TPU:0, one launch (start us, length us, event | category | flops | bytes accessed | tf_op | source)
XLA Modules:
  0.0 178.0 jit_solution(4584738750597114198)
XLA Ops:
  0.7 0.9 convert_element_type.89
  1.5 1.1 fusion.52
  2.7 1.4 convolution_convert_fusion.3
  4.1 4.6 %convolution_convert_fusion.2 = bf16[16,512]{1,0:T(8,128)(2,1)S(1)} fusion(bf16[8192,512]{1,0:T(8,128)(2,1)} %param.17, bf16[16,8192]{1,0:T(8,128)(2,1)S(1)} %copy-done.1, f32[8192]{0:T(1024)S(1)} %convert_element_type.89, f32[16]{0:T(128)S(1)} %add_rsqrt_fusion.1), kind=kOutput, calls=%fused_computation.23 | convolution fusion | flops 134750208 | bytes 8699968 | tf_op jit(solution)/shard_map/dot_general | solution.py:103
  8.7 0.6 pad_maximum_fusion.1
  9.4 7.3 %all-to-all-start = ((bf16[8,2,640]{2,1,0:T(2,128)(2,1)}), bf16[8,2,640]{2,1,0:T(2,128)(2,1)S(1)}, u32[]{:S(2)}, u32[]{:S(2)}) async-start(bf16[8,2,640]{2,1,0:T(2,128)(2,1)} %pad_maximum_fusion.1), calls=%async_computation | async-start | bytes 40960 | tf_op jit(solution)/shard_map/all_to_all | solution.py:89
  17.3 0.7 dynamic-slice.10
  18.1 3.0 %fusion.98 = (bf16[2,512,512]{2,1,0:T(8,128)(2,1)}, bf16[2,512,512]{2,1,0:T(8,128)(2,1)}) fusion(bf16[2,512,1024]{2,1,0:T(8,128)(2,1)} %param.20), kind=kLoop, calls=%fused_computation.144 | loop fusion | bytes 4194304 | tf_op jit(solution)/shard_map/slice | solution.py:79
  21.1 1.5 copy.123
  22.6 1.3 copy.102
  23.9 1.5 copy.122
  25.4 1.3 copy.100
  28.1 0.7 multiply_cosine_fusion
  29.5 1.4 dynamic-slice_select_fusion.1
  30.9 0.6 stack_reshape.10
  31.6 0.6 copy.99
  32.8 0.7 fusion.74
  33.6 2.4 %fusion.99 = (f32[2,4,8]{2,1,0:T(4,128)S(1)}, f32[2,4,8,513]{3,2,1,0:T(8,128)}) fusion(bf16[2,1,4,64]{3,1,2,0:T(2,128)(2,1)} %copy.99, bf16[2,1,4,64]{3,1,2,0:T(2,128)(2,1)} %copy.98, bf16[2,512,4,128]{3,1,2,0:T(8,128)(2,1)} %copy.100, pred[2,513]{1,0:T(4,128)(4,1)} %concatenate.98, bf16[2,4,8,64]{3,2,1,0:T(8,128)(2,1)S(1)} %get-tuple-element.48, ...), kind=kOutput, calls=%fused_computation.145 | convolution fusion | flops 11754304 | bytes 1199618 | tf_op jit(solution)/shard_map/sub | solution.py:134
  36.0 1.2 convolution_convert_fusion.1
  37.3 0.6 copy.153
  37.9 6.0 %all-to-all-start.1 = ((bf16[8,2,512]{2,1,0:T(2,128)(2,1)}), bf16[8,2,512]{2,1,0:T(2,128)(2,1)S(1)}, u32[]{:S(2)}, u32[]{:S(2)}) async-start(bf16[8,2,512]{2,1,0:T(2,128)(2,1)} %bitcast.105), calls=%async_computation.1 | async-start | bytes 32768 | tf_op jit(solution)/shard_map/all_to_all | solution.py:89
  43.9 0.7 dynamic-slice_select_fusion.3
  44.6 5.8 %all-to-all-done.1 = bf16[8,2,512]{2,1,0:T(2,128)(2,1)S(1)} async-done(((bf16[8,2,512]{2,1,0:T(2,128)(2,1)}), bf16[8,2,512]{2,1,0:T(2,128)(2,1)S(1)}, u32[]{:S(2)}, u32[]{:S(2)}) %all-to-all-start.1) | async-done | bytes 16416 | tf_op jit(solution)/shard_map/all_to_all | solution.py:89
  50.5 4.6 %fusion.6 = f32[8,2,8192]{2,0,1:T(8,128)S(1)} fusion(bf16[512,8192]{1,0:T(8,128)(2,1)} %param.19, bf16[8,2,512]{2,1,0:T(2,128)(2,1)S(1)} %all-to-all-done.1), kind=kOutput, calls=%fused_computation.6 | convolution fusion | flops 134217728 | bytes 8929280 | tf_op jit(solution)/shard_map/dot_general | solution.py:152
  55.0 1.2 copy.107
  56.2 3.5 %all-to-all-start.2 = ((f32[8,2,8192]{2,1,0:T(2,128)}), f32[8,2,8192]{2,1,0:T(2,128)S(1)}, u32[]{:S(2)}, u32[]{:S(2)}) async-start(f32[8,2,8192]{2,1,0:T(2,128)} %copy.107), calls=%async_computation.2 | async-start | bytes 1048576 | tf_op jit(solution)/shard_map/all_to_all | solution.py:89
  62.7 34.7 %all-gather = bf16[8,16,1536]{2,1,0:T(8,128)(2,1)S(1)} all-gather(bf16[1,16,1536]{2,1,0:T(8,128)(2,1)S(1)} %maximum_select_fusion), channel_id=2, replica_groups=mesh['parts'=2,'req'=2,'tp'=8] {'tp'}, dimensions={0}, use_global_device_ids=true | all-gather | bytes 442368 | tf_op jit(solution)/shard_map/all_gather | solution.py:50
  98.4 10.6 %all_to_all.40 = bf16[8,2,8192]{2,1,0:T(2,128)(2,1)S(1)} all-to-all(bf16[8,2,8192]{2,1,0:T(2,128)(2,1)S(1)} %broadcast_in_dim.109), channel_id=1, replica_groups=mesh['parts'=2,'req'=2,'tp'=8] {'tp'}, dimensions={0} | all-to-all | bytes 524288 | tf_op jit(solution)/shard_map/all_to_all | solution.py:89
  109.5 4.6 %fusion.18 = bf16[8,2,512]{2,0,1:T(8,128)(2,1)S(1)} fusion(bf16[8192,512]{1,0:T(8,128)(2,1)} %param.17, bf16[8,2,8192]{2,1,0:T(2,128)(2,1)S(1)} %all_to_all.40), kind=kOutput, calls=%fused_computation.20 | convolution fusion | flops 134225920 | bytes 8667136 | tf_op jit(solution)/shard_map/dot_general | solution.py:103
  114.1 0.6 copy.110
  114.7 3.3 %all-to-all-start.4 = ((bf16[8,2,640]{2,1,0:T(2,128)(2,1)}), bf16[8,2,640]{2,1,0:T(2,128)(2,1)S(1)}, u32[]{:S(2)}, u32[]{:S(2)}) async-start(bf16[8,2,640]{2,1,0:T(2,128)(2,1)} %copy.110), calls=%async_computation.4 | async-start | bytes 40960 | tf_op jit(solution)/shard_map/all_to_all | solution.py:89
  118.1 0.6 concatenate.112
  118.7 5.9 %all-to-all-done.4 = bf16[8,2,640]{2,1,0:T(2,128)(2,1)S(1)} async-done(((bf16[8,2,640]{2,1,0:T(2,128)(2,1)}), bf16[8,2,640]{2,1,0:T(2,128)(2,1)S(1)}, u32[]{:S(2)}, u32[]{:S(2)}) %all-to-all-start.4) | async-done | bytes 20512 | tf_op jit(solution)/shard_map/all_to_all | solution.py:89
  125.4 0.6 copy.113
  126.6 0.7 fusion.76
  127.2 3.1 %fusion.102 = (f32[2,4,8]{2,1,0:T(4,128)}, f32[2,4,8,514]{3,2,1,0:T(8,128)}) fusion(pred[2,514]{1,0:T(4,128)(4,1)} %concatenate.112, bf16[2,1,4,64]{3,1,2,0:T(2,128)(2,1)} %copy.113, bf16[2,1,4,64]{3,1,2,0:T(2,128)(2,1)} %copy.112, bf16[2,1,4,64]{3,1,2,0:T(2,128)(2,1)} %copy.99, bf16[2,1,4,64]{3,1,2,0:T(2,128)(2,1)} %copy.98, ...), kind=kOutput, calls=%fused_computation.146 | convolution fusion | flops 13882497 | bytes 1201924 | tf_op jit(solution)/shard_map/sub | solution.py:134
  130.4 1.8 %convolution_convert_fusion = bf16[2,4,8,128]{3,2,1,0:T(8,128)(2,1)} fusion(bf16[2,1,4,128]{3,1,2,0:T(2,128)(2,1)} %stack_reshape.9, bf16[2,1,4,128]{3,1,2,0:T(2,128)(2,1)} %stack_reshape.10, bf16[2,512,4,128]{3,1,2,0:T(8,128)(2,1)S(1)} %copy-done.3, f32[2,4,8,514]{3,2,1,0:T(8,128)} %get-tuple-element.68, f32[2,4,8]{2,1,0:T(4,128)} %get-tuple-element.67), kind=kOutput, calls=%fused_computation.21 | convolution fusion | flops 11653376 | bytes 1200896 | tf_op jit(solution)/shard_map/rkgp,rpkd->rkgd/dot_general | solution.py:138
  132.2 0.7 reshape.335
  133.0 8.9 %all_to_all.41 = bf16[8,2,512]{2,1,0:T(2,128)(2,1)S(1)} all-to-all(bf16[8,2,512]{2,1,0:T(2,128)(2,1)S(1)} %bitcast.118), channel_id=1, replica_groups=mesh['parts'=2,'req'=2,'tp'=8] {'tp'}, dimensions={0} | all-to-all | bytes 32768 | tf_op jit(solution)/shard_map/all_to_all | solution.py:89
  141.9 4.6 %fusion.4 = f32[8,2,8192]{2,0,1:T(8,128)S(1)} fusion(bf16[512,8192]{1,0:T(8,128)(2,1)} %param.19, bf16[8,2,512]{2,1,0:T(2,128)(2,1)S(1)} %all_to_all.41), kind=kOutput, calls=%fused_computation.4 | convolution fusion | flops 134217728 | bytes 8929280 | tf_op jit(solution)/shard_map/dot_general | solution.py:152
  146.5 1.2 copy.121
  147.7 3.5 %all-to-all-start.6 = ((f32[8,2,8192]{2,1,0:T(2,128)}), f32[8,2,8192]{2,1,0:T(2,128)S(1)}, u32[]{:S(2)}, u32[]{:S(2)}) async-start(f32[8,2,8192]{2,1,0:T(2,128)} %copy.121), calls=%async_computation.6 | async-start | bytes 1048576 | tf_op jit(solution)/shard_map/all_to_all | solution.py:89
  151.6 11.6 %all-to-all-done.6 = f32[8,2,8192]{2,1,0:T(2,128)S(1)} async-done(((f32[8,2,8192]{2,1,0:T(2,128)}), f32[8,2,8192]{2,1,0:T(2,128)S(1)}, u32[]{:S(2)}, u32[]{:S(2)}) %all-to-all-start.6) | async-done | bytes 524320 | tf_op jit(solution)/shard_map/all_to_all | solution.py:89
  163.5 0.8 broadcast_in_dim.112
  164.3 4.7 %all-to-all-start.7 = ((bf16[8,2,8192]{2,1,0:T(2,128)(2,1)}), bf16[8,2,8192]{2,1,0:T(2,128)(2,1)S(1)}, u32[]{:S(2)}, u32[]{:S(2)}) async-start(bf16[8,2,8192]{2,1,0:T(2,128)(2,1)} %broadcast_in_dim.112), calls=%async_computation.7 | async-start | bytes 524288 | tf_op jit(solution)/shard_map/all_to_all | solution.py:89
  169.2 0.6 pad_maximum_fusion.4
  169.8 7.4 %all-to-all-done.7 = bf16[8,2,8192]{2,1,0:T(2,128)(2,1)S(1)} async-done(((bf16[8,2,8192]{2,1,0:T(2,128)(2,1)}), bf16[8,2,8192]{2,1,0:T(2,128)(2,1)S(1)}, u32[]{:S(2)}, u32[]{:S(2)}) %all-to-all-start.7) | async-done | bytes 262176 | tf_op jit(solution)/shard_map/all_to_all | solution.py:89
  177.2 0.8 reshape.337
  (85 shorter events, 5.2 us)
Async XLA Ops:
  0.6 2.0 %copy-start = (bf16[8192,128]{1,0:T(8,128)(2,1)S(1)}, bf16[8192,128]{1,0:T(8,128)(2,1)}, u32[]{:S(2)}) copy-start(bf16[8192,128]{1,0:T(8,128)(2,1)} %param.18) | copy-start | bytes 6291460
  0.6 3.4 %copy-start.1 = (bf16[16,8192]{1,0:T(8,128)(2,1)S(1)}, bf16[16,8192]{1,0:T(8,128)(2,1)}, u32[]{:S(2)}) copy-start(bf16[16,8192]{1,0:T(8,128)(2,1)} %param.15) | copy-start | bytes 786436
  4.1 13.2 %copy-start.16 = (s32[128]{0:T(128)S(1)}, s32[128]{0:T(128)}, u32[]{:S(2)}) copy-start(s32[128]{0:T(128)} %param.23) | copy-start | bytes 1540
  4.1 13.9 %copy-start.15 = (s32[2]{0:T(128)S(1)}, s32[2]{0:T(128)}, u32[]{:S(2)}) copy-start(s32[2]{0:T(128)} %param.21) | copy-start | bytes 28
  9.4 21.5 %all-to-all-start = ((bf16[8,2,640]{2,1,0:T(2,128)(2,1)}), bf16[8,2,640]{2,1,0:T(2,128)(2,1)S(1)}, u32[]{:S(2)}, u32[]{:S(2)}) async-start(bf16[8,2,640]{2,1,0:T(2,128)(2,1)} %pad_maximum_fusion.1), calls=%async_computation | async-start | bytes 40960 | tf_op jit(solution)/shard_map/all_to_all | solution.py:89
  18.0 10.8 %collective-permute-start = (s32[1]{0:T(128)}, s32[1]{0:T(128)}, u32[]{:S(2)}, u32[]{:S(2)}) collective-permute-start(s32[1]{0:T(128)} %dynamic-slice.10), channel_id=1, source_target_pairs={{0,8},{8,0},{1,9},{9,1},{2,10},{10,2},{3,11},{11,3},{4,12},{12,4},... | collective-permute-start | bytes 20 | tf_op jit(solution)/shard_map/ppermute | solution.py:42
  26.8 9.3 %copy-start.2 = (bf16[2,512,4,128]{3,1,2,0:T(8,128)(2,1)S(1)}, bf16[2,512,4,128]{3,1,2,0:T(8,128)(2,1)}, u32[]{:S(2)}) copy-start(bf16[2,512,4,128]{3,1,2,0:T(8,128)(2,1)} %copy.102) | copy-start | bytes 3145732
  28.8 3.4 %copy-start.13 = (f32[2,64]{1,0:T(2,128)}, f32[2,64]{1,0:T(2,128)S(1)}, u32[]{:S(2)}) copy-start(f32[2,64]{1,0:T(2,128)S(1)} %get-tuple-element.62) | copy-start | bytes 1540
  30.9 0.6 copy-start.7
  33.6 2.4 %copy-start.14 = (bf16[2,1,4,128]{3,1,2,0:T(2,128)(2,1)S(1)}, bf16[2,1,4,128]{3,1,2,0:T(2,128)(2,1)}, u32[]{:S(2)}) copy-start(bf16[2,1,4,128]{3,1,2,0:T(2,128)(2,1)} %stack_reshape.10) | copy-start | bytes 6148
  37.9 12.6 %all-to-all-start.1 = ((bf16[8,2,512]{2,1,0:T(2,128)(2,1)}), bf16[8,2,512]{2,1,0:T(2,128)(2,1)S(1)}, u32[]{:S(2)}, u32[]{:S(2)}) async-start(bf16[8,2,512]{2,1,0:T(2,128)(2,1)} %bitcast.105), calls=%async_computation.1 | async-start | bytes 32768 | tf_op jit(solution)/shard_map/all_to_all | solution.py:89
  55.0 7.6 %copy-start.6 = (bf16[1,16,1024]{2,1,0:T(8,128)(2,1)S(1)}, bf16[1,16,1024]{2,1,0:T(8,128)(2,1)}, u32[]{:S(2)}) copy-start(bf16[1,16,1024]{2,1,0:T(8,128)(2,1)} %get-tuple-element.39) | copy-start | bytes 98308
  56.2 41.4 %all-to-all-start.2 = ((f32[8,2,8192]{2,1,0:T(2,128)}), f32[8,2,8192]{2,1,0:T(2,128)S(1)}, u32[]{:S(2)}, u32[]{:S(2)}) async-start(f32[8,2,8192]{2,1,0:T(2,128)} %copy.107), calls=%async_computation.2 | async-start | bytes 1048576 | tf_op jit(solution)/shard_map/all_to_all | solution.py:89
  59.8 2.9 %collective-permute-start.1 = (bf16[1,16,1536]{2,1,0:T(8,128)(2,1)S(1)}, bf16[1,16,1536]{2,1,0:T(8,128)(2,1)S(1)}, u32[]{:S(2)}, u32[]{:S(2)}) collective-permute-start(bf16[1,16,1536]{2,1,0:T(8,128)(2,1)S(1)} %pad_maximum_fusion), channel_id=1, source_target_pairs={{0,8},{8,0},{1,9},{9,1},{2,10},{10,2},{3,11},{11,3},{4,12},{12,4},... | collective-permute-start | bytes 147464 | tf_op jit(solution)/shard_map/ppermute | solution.py:48
  98.1 16.0 %copy-start.4 = (bf16[2,8192]{1,0:T(2,128)(2,1)}, bf16[2,8192]{1,0:T(2,128)(2,1)S(1)}, u32[]{:S(2)}) copy-start(bf16[2,8192]{1,0:T(2,128)(2,1)S(1)} %get-tuple-element.38) | copy-start | bytes 98308
  109.5 15.8 %copy-start.11 = (f32[2,64]{1,0:T(2,128)S(1)}, f32[2,64]{1,0:T(2,128)}, u32[]{:S(2)}) copy-start(f32[2,64]{1,0:T(2,128)} %get-tuple-element.57) | copy-start | bytes 1540
  109.5 15.8 %copy-start.12 = (f32[2,64]{1,0:T(2,128)S(1)}, f32[2,64]{1,0:T(2,128)}, u32[]{:S(2)}) copy-start(f32[2,64]{1,0:T(2,128)} %get-tuple-element.58) | copy-start | bytes 1540
  114.7 9.9 %all-to-all-start.4 = ((bf16[8,2,640]{2,1,0:T(2,128)(2,1)}), bf16[8,2,640]{2,1,0:T(2,128)(2,1)S(1)}, u32[]{:S(2)}, u32[]{:S(2)}) async-start(bf16[8,2,640]{2,1,0:T(2,128)(2,1)} %copy.110), calls=%async_computation.4 | async-start | bytes 40960 | tf_op jit(solution)/shard_map/all_to_all | solution.py:89
  124.7 0.6 copy-start.9
  127.2 3.1 %copy-start.3 = (bf16[2,512,4,128]{3,1,2,0:T(8,128)(2,1)S(1)}, bf16[2,512,4,128]{3,1,2,0:T(8,128)(2,1)}, u32[]{:S(2)}) copy-start(bf16[2,512,4,128]{3,1,2,0:T(8,128)(2,1)} %copy.102) | copy-start | bytes 3145732
  146.5 16.9 %copy-start.5 = (bf16[2,8192]{1,0:T(2,128)(2,1)S(1)}, bf16[2,8192]{1,0:T(2,128)(2,1)}, u32[]{:S(2)}) copy-start(bf16[2,8192]{1,0:T(2,128)(2,1)} %copy-done.4) | copy-start | bytes 98308
  146.5 22.7 %copy-start.8 = (bf16[2,512]{1,0:T(2,128)(2,1)S(1)}, bf16[2,512]{1,0:T(2,128)(2,1)}, u32[]{:S(2)}) copy-start(bf16[2,512]{1,0:T(2,128)(2,1)} %copy-done.7) | copy-start | bytes 6148
  146.5 22.7 %copy-start.10 = (bf16[2,512]{1,0:T(2,128)(2,1)S(1)}, bf16[2,512]{1,0:T(2,128)(2,1)}, u32[]{:S(2)}) copy-start(bf16[2,512]{1,0:T(2,128)(2,1)} %copy-done.9) | copy-start | bytes 6148
  147.7 15.5 %all-to-all-start.6 = ((f32[8,2,8192]{2,1,0:T(2,128)}), f32[8,2,8192]{2,1,0:T(2,128)S(1)}, u32[]{:S(2)}, u32[]{:S(2)}) async-start(f32[8,2,8192]{2,1,0:T(2,128)} %copy.121), calls=%async_computation.6 | async-start | bytes 1048576 | tf_op jit(solution)/shard_map/all_to_all | solution.py:89
  164.3 12.9 %all-to-all-start.7 = ((bf16[8,2,8192]{2,1,0:T(2,128)(2,1)}), bf16[8,2,8192]{2,1,0:T(2,128)(2,1)S(1)}, u32[]{:S(2)}, u32[]{:S(2)}) async-start(bf16[8,2,8192]{2,1,0:T(2,128)(2,1)} %broadcast_in_dim.112), calls=%async_computation.7 | async-start | bytes 524288 | tf_op jit(solution)/shard_map/all_to_all | solution.py:89

commit v2 on v1

v2 whole, which is shorter than its diff:
```python
import math

import jax
import jax.numpy as jnp
from jax import lax
from jax.experimental import pallas as pl
from jax.experimental.pallas import tpu as pltpu
from jax.sharding import PartitionSpec as P

MODEL_WIDTH = 8192
HEAD_SIZE = 128
QUERY_HEAD_COUNT = 32
KV_HEADS = 4
BLOCK = 16
STEPS = 2

rope_base = 500000.0
norm_epsilon = 1e-05
term_type = jnp.float32
f32 = jnp.float32
bf16 = jnp.bfloat16
MIB = 1 << 20


def whole(kind=pltpu.VMEM):
    return pl.BlockSpec(memory_space=kind)


def call(body, outs, ins, flops, data_bytes, limit=48):
    return pl.pallas_call(
        body,
        out_shape=outs,
        in_specs=ins,
        out_specs=jax.tree.map(lambda _: whole(), outs),
        compiler_params=pltpu.CompilerParams(vmem_limit_bytes=limit * MIB),
        cost_estimate=pl.CostEstimate(flops=flops, bytes_accessed=data_bytes, transcendentals=0),
    )


def rows_of(ref, start, width):
    pieces = [ref[j, :, pl.ds(start, width)].astype(f32) for j in range(ref.shape[0])]
    return jnp.concatenate(pieces, axis=0).astype(bf16)


def project(source, query_weight, pair_weight, chunk_of, shares):
    depth, query_width = query_weight.shape
    pair_width = pair_weight.shape[1]
    step = 512

    def loop(i, sums):
        at = pl.multiple_of(i * step, step)
        part = chunk_of(at, step)
        rows = pl.ds(at, step)
        return (
            sums[0] + jnp.dot(part, query_weight[rows, :], preferred_element_type=f32),
            sums[1] + jnp.dot(part, pair_weight[rows, :], preferred_element_type=f32),
        )

    count = shares[0] * shares[1]
    zero = (jnp.zeros((count, query_width), f32), jnp.zeros((count, pair_width), f32))
    return lax.fori_loop(0, depth // step, loop, zero, unroll=2)


def store_shares(out, query, pair):
    shares, own, _ = out.shape
    width = query.shape[1]
    for j in range(shares):
        out[j, :, :width] = query[j * own : (j + 1) * own].astype(bf16)
        out[j, :, width:] = pair[j * own : (j + 1) * own].astype(bf16)


def first_projection(hidden, scale, query_weight, pair_weight, own):
    rows, width = hidden.shape
    shares = rows // own

    def body(h, s, wq, wp, out, normed):
        wide = h[...].astype(f32)
        mean = jnp.mean(wide * wide, axis=-1, keepdims=True)
        normed[...] = (wide * lax.rsqrt(mean + norm_epsilon) * s[...].astype(f32)).astype(bf16)
        sums = project(
            h, wq, wp, lambda at, n: normed[:, pl.ds(at, n)], (shares, own)
        )
        store_shares(out, *sums)

    message = query_weight.shape[1] + pair_weight.shape[1]
    return pl.pallas_call(
        body,
        out_shape=jax.ShapeDtypeStruct((shares, own, message), bf16),
        in_specs=[whole()] * 4,
        out_specs=whole(),
        scratch_shapes=[pltpu.VMEM((rows, width), bf16)],
        compiler_params=pltpu.CompilerParams(vmem_limit_bytes=48 * MIB),
        cost_estimate=pl.CostEstimate(
            flops=2 * rows * width * message, bytes_accessed=2 * width * message, transcendentals=0
        ),
    )(hidden, scale, query_weight, pair_weight)


def next_projection(normed, query_weight, pair_weight):
    shares, own, width = normed.shape

    def body(x, wq, wp, out):
        sums = project(x, wq, wp, lambda at, n: rows_of(x, at, n), (shares, own))
        store_shares(out, *sums)

    message = query_weight.shape[1] + pair_weight.shape[1]
    return call(
        body,
        jax.ShapeDtypeStruct((shares, own, message), bf16),
        [whole()] * 3,
        2 * shares * own * width * message,
        2 * width * message,
    )(normed, query_weight, pair_weight)


def attend(arrived, pairs, older, angles, lengths, cache, down, step):
    shares, own, message = arrived.shape
    context, width = cache.shape[1:]
    half = width // 2
    query_width = QUERY_HEAD_COUNT * HEAD_SIZE // shares
    per_share = query_width // HEAD_SIZE
    groups = QUERY_HEAD_COUNT // KV_HEADS
    pair_inside = pairs is None
    rank = down.shape[1]

    def body(*refs):
        refs = list(refs)
        lens, x = refs.pop(0), refs.pop(0)
        pair_ref = None if pair_inside else refs.pop(0)
        old = refs.pop(0) if step else None
        cos_ref, sin_ref, kv, down_ref, out, new = refs
        place = lax.broadcasted_iota(jnp.int32, (groups, context), 1)
        rows = [x[j].astype(f32) for j in range(shares)]
        outputs = []
        fresh = []
        for r in range(own):
            cosine = cos_ref[r : r + 1, :]
            sine = sin_ref[r : r + 1, :]

            def turn(v):
                return v * cosine + pltpu.roll(v, HEAD_SIZE // 2, 1) * sine

            def pair_head(c):
                if pair_inside:
                    return rows[c][r : r + 1, query_width:]
                return pair_ref[r : r + 1, c * HEAD_SIZE : (c + 1) * HEAD_SIZE].astype(f32)

            heads = []
            line = []
            for g in range(KV_HEADS):
                line.append(turn(pair_head(g)).astype(bf16))
            for g in range(KV_HEADS):
                line.append(pair_head(KV_HEADS + g).astype(bf16))
            fresh.append(jnp.concatenate([v.astype(f32) for v in line], axis=1))
            for g in range(KV_HEADS):
                column = slice(g * HEAD_SIZE, (g + 1) * HEAD_SIZE)
                value_column = slice(half + g * HEAD_SIZE, half + (g + 1) * HEAD_SIZE)
                lines = []
                for h in range(g * groups, (g + 1) * groups):
                    at = (h % per_share) * HEAD_SIZE
                    lines.append(rows[h // per_share][r : r + 1, at : at + HEAD_SIZE])
                query = turn(jnp.concatenate(lines, axis=0)).astype(bf16)
                scores = lax.dot_general(
                    query, kv[r, :, column], (((1,), (1,)), ((), ())), preferred_element_type=f32
                ) * (1.0 / math.sqrt(HEAD_SIZE))
                scores = jnp.where(place < lens[r], scores, f32(-1e30))
                new_keys = [line[g].astype(f32)]
                new_values = [line[KV_HEADS + g].astype(f32)]
                if step:
                    new_keys.append(old[r : r + 1, column].astype(f32))
                    new_values.append(old[r : r + 1, value_column].astype(f32))
                wide_query = query.astype(f32)
                extra = [
                    jnp.sum(wide_query * k, axis=1, keepdims=True) * (1.0 / math.sqrt(HEAD_SIZE))
                    for k in new_keys
                ]
                peak = jnp.max(scores, axis=1, keepdims=True)
                for e in extra:
                    peak = jnp.maximum(peak, e)
                weight = jnp.exp(scores - peak)
                extra = [jnp.exp(e - peak) for e in extra]
                total = jnp.sum(weight, axis=1, keepdims=True)
                for e in extra:
                    total = total + e
                result = jnp.dot(
                    (weight / total).astype(bf16), kv[r, :, value_column], preferred_element_type=f32
                )
                for e, v in zip(extra, new_values):
                    result = result + (e / total).astype(bf16).astype(f32) * v
                heads.append(result)
            outputs.append(heads)
        new[...] = jnp.concatenate(fresh, axis=0).astype(bf16)
        low = jnp.zeros((own, rank), f32)
        for j in range(shares):
            lines = []
            for r in range(own):
                cells = []
                for h in range(j * per_share, (j + 1) * per_share):
                    at = h % groups
                    cells.append(outputs[r][h // groups][at : at + 1, :])
                lines.append(jnp.concatenate(cells, axis=1))
            share = jnp.concatenate(lines, axis=0).astype(bf16)
            out[j, :, :query_width] = share
            low = low + lax.dot_general(
                share, down_ref[j], (((1,), (1,)), ((), ())), preferred_element_type=f32
            )
        padded = jnp.concatenate([low, jnp.zeros((own, HEAD_SIZE - rank), f32)], axis=1).astype(bf16)
        for j in range(shares):
            out[j, :, query_width:] = padded

    operands = [lengths, arrived]
    specs = [whole(pltpu.SMEM), whole()]
    for extra in ([] if pair_inside else [pairs]) + ([older] if step else []):
        operands.append(extra)
        specs.append(whole())
    operands += [angles[0], angles[1], cache, down]
    specs += [whole()] * 4
    return call(
        body,
        (
            jax.ShapeDtypeStruct((shares, own, query_width + HEAD_SIZE), bf16),
            jax.ShapeDtypeStruct((own, width), bf16),
        ),
        specs,
        8 * own * QUERY_HEAD_COUNT * HEAD_SIZE * context,
        2 * own * context * width,
    )(*operands)


def output_terms(arrived, output_weight, up, blocks):
    shares, own, _ = arrived.shape
    query_width, width = output_weight.shape
    share_width = up.shape[2]
    rank = up.shape[1]
    rows = shares * own
    step = 1024

    def body(mine, x, wo, up_ref, out, total):
        heads = rows_of(x, 0, query_width)
        low = rows_of(x, query_width, HEAD_SIZE)[:, :rank]

        def loop(i, carry):
            at = pl.multiple_of(i * step, step)
            total[:, pl.ds(at, step)] = jnp.dot(
                heads, wo[:, pl.ds(at, step)], preferred_element_type=f32
            )
            return carry

        lax.fori_loop(0, width // step, loop, 0)
        start = pl.multiple_of(mine[0] * share_width, share_width)
        for b in range(blocks):
            lines = slice(b * BLOCK, (b + 1) * BLOCK)
            total[lines, pl.ds(start, share_width)] += jnp.dot(
                low[lines], up_ref[b], preferred_element_type=f32
            )
        for j in range(shares):
            out[j] = total[j * own : (j + 1) * own, :].astype(out.dtype)

    return pl.pallas_call(
        body,
        out_shape=jax.ShapeDtypeStruct((shares, own, width), term_type),
        in_specs=[whole(pltpu.SMEM)] + [whole()] * 3,
        out_specs=whole(),
        scratch_shapes=[pltpu.VMEM((rows, width), f32)],
        compiler_params=pltpu.CompilerParams(vmem_limit_bytes=48 * MIB),
        cost_estimate=pl.CostEstimate(
            flops=2 * rows * width * query_width,
            bytes_accessed=2 * width * query_width,
            transcendentals=0,
        ),
    )(lax.axis_index("tp").astype(jnp.int32).reshape(1), arrived, output_weight, up)


def close_step(terms, hidden, scale):
    shares, own, width = terms.shape
    normed = scale is not None

    def body(t, h, *refs):
        total = h[...].astype(f32)
        for j in range(shares):
            total = total + t[j].astype(f32)
        rounded = total.astype(bf16)
        spread = rounded
        if normed:
            s, out, kept = refs
            kept[...] = rounded
            wide = rounded.astype(f32)
            mean = jnp.mean(wide * wide, axis=-1, keepdims=True)
            spread = (wide * lax.rsqrt(mean + norm_epsilon) * s[...].astype(f32)).astype(bf16)
        else:
            (out,) = refs
        for j in range(shares):
            out[j] = spread

    outs = [jax.ShapeDtypeStruct((shares, own, width), bf16)]
    operands = [terms, hidden]
    if normed:
        outs.append(jax.ShapeDtypeStruct((own, width), bf16))
        operands.append(scale)
    return call(
        body, tuple(outs), [whole()] * len(operands), 8 * own * width, 6 * shares * own * width
    )(*operands)


def block_adapters(adapter_per_block, adapter_storage_slot, down, up):
    own = lax.axis_index("req")
    stored_here = down.shape[0]
    slot = adapter_storage_slot[adapter_per_block]
    other_slot = lax.ppermute(slot, "req", [(0, 1), (1, 0)])

    def piece(which):
        at = jnp.clip(which - own * stored_here, 0, stored_here - 1)
        return jnp.concatenate([jnp.take(down, at, axis=0), jnp.take(up, at, axis=0)], axis=2)

    sent = lax.ppermute(piece(other_slot), "req", [(0, 1), (1, 0)])
    held = jnp.where((slot // stored_here == own)[:, None, None], piece(slot), sent)
    return held[:, :, : down.shape[2]], held[:, :, down.shape[2] :]


def exchange(chunks):
    return lax.all_to_all(chunks, "tp", split_axis=0, concat_axis=0, tiled=True)


def local(
    input_hidden_rows,
    input_norm_scale,
    query_weight,
    key_value_weight,
    output_weight,
    cache,
    lengths,
    adapter_per_block,
    adapter_storage_slot,
    adapter_down_projection,
    adapter_up_projection,
):
    tp_count = lax.axis_size("tp")
    tp_index = lax.axis_index("tp")
    rows_req = input_hidden_rows.shape[0]
    own = cache.shape[0]
    blocks = rows_req // BLOCK
    width = input_hidden_rows.shape[1]
    query_width = query_weight.shape[1]
    scale = input_norm_scale.reshape(1, width)
    down, up = block_adapters(
        adapter_per_block, adapter_storage_slot, adapter_down_projection, adapter_up_projection
    )
    down_chunks = jnp.repeat(down, tp_count // blocks, axis=0)
    down_own = exchange(down_chunks)
    half_head = HEAD_SIZE // 2
    frequency = rope_base ** (-(jnp.arange(half_head, dtype=f32) * 2.0 / HEAD_SIZE))
    hidden = lax.dynamic_slice_in_dim(input_hidden_rows, tp_index * own, own, 0)
    stored = []
    message = first_projection(input_hidden_rows, scale, query_weight, key_value_weight, own)
    for step in range(STEPS):
        angle = (lengths + step).astype(f32)[:, None] * frequency[None, :]
        cosine, sine = jnp.cos(angle), jnp.sin(angle)
        angles = (
            jnp.concatenate([cosine, cosine], axis=1),
            jnp.concatenate([-sine, sine], axis=1),
        )
        arrived = exchange(message)
        pairs = None
        if key_value_weight.shape[1] != HEAD_SIZE:
            pairs = arrived[:, :, query_width:].transpose(1, 0, 2).reshape(own, -1)
        attended, fresh = attend(
            arrived, pairs, stored[-1] if step else None, angles, lengths, cache, down_own, step
        )
        stored.append(fresh)
        terms = exchange(output_terms(exchange(attended), output_weight, up, blocks))
        if step < STEPS - 1:
            spread, hidden = close_step(terms, hidden, scale)
            message = next_projection(exchange(spread), query_weight, key_value_weight)
        else:
            (spread,) = close_step(terms, hidden, None)
    return (exchange(spread).reshape(rows_req, width), jnp.stack(stored, axis=0))


def solution(mesh):
    in_specs = (
        P(("parts", "req"), None),
        P(),
        P(None, "tp"),
        P(None, "tp"),
        P("tp", None),
        P(("parts", "req", "tp"), None, None),
        P(("parts", "req", "tp")),
        P(("parts", "req")),
        P(),
        P("req", None, "tp"),
        P("req", None, "tp"),
    )
    out_specs = (P(("parts", "req"), None), P(None, ("parts", "req", "tp"), None))
    return jax.shard_map(local, mesh=mesh, in_specs=in_specs, out_specs=out_specs, check_vma=False)
```

time: 179 us -> 153 us (0.85)
  Pallas kernels: 0 us -> 33.6 us
  matrix products: 29.6 us -> 0 us
  blocking collectives: 54.2 us -> 34.6 us
  local copies, waits for them, and re-layouts: 20.4 us -> 8.61 us
  waiting for transfers between devices: 30.8 us -> 40.5 us
  other arithmetic: 8.71 us -> 2.45 us
    all_gather x1 -> x0, blocking collectives: 34.7 us -> none  [row_adapters(): gathered = lax.all_gather(held, 'tp', axis=0, tiled=False)]
    pallas_call x0 -> x8, Pallas kernels: none -> 33.6 us  [the longest x2 12.1 us: output_terms(): pl.pallas_call(body, out_shape=jax.ShapeDtypeStruct((shares, own, width),...]
    dot_general x10 -> x0, matrix products: 24 us -> none  [the longest x2 9.18 us: local(): jnp.dot(normed, query_weight, preferred_element_type=jnp.float32)]
    all_to_all x2 -> x3, blocking collectives: 19.6 us -> 34.6 us  [exchange(): return lax.all_to_all(chunks, 'tp', split_axis=0, concat_axis=0, tiled=True)]
    all_to_all x6, waiting for transfers between devices: 30.8 us -> 40.5 us  [exchange(): return lax.all_to_all(chunks, 'tp', split_axis=0, concat_axis=0, tiled=True)]
    sub x2 -> x0, matrix products: 5.57 us -> none  [local(): scores - row_peak]
    concatenate x8 -> x0, local copies, waits for them, and re-layouts: 4.19 us -> none  [the longest x4 2.37 us: rotate(): jnp.concatenate([front_half * cosine - back_half * sine_part, back_half *...]
    slice x1 -> x2, local copies, waits for them, and re-layouts: 3.01 us -> 0.01 us  [block_adapters(): return (held[:, :, :down.shape[2]], held[:, :, down.shape[2]:])]
  transfers between devices with their start and end apart: 8 -> 8, of which waited for: 4 -> 6; matrix products, arithmetic and copies ran while one was open for 8% -> 3% of each run, Pallas kernels for 0% -> 4%
where the time goes in v2:
time: 153 us; the launch traced here: 152 us
  waiting for transfers between devices  40.5 us (26%)
  blocking collectives  34.6 us (23%)
  Pallas kernels  33.6 us (22%)
  starting transfers between devices  26.8 us (18%)
  local copies, waits for them, and re-layouts  8.61 us (6%)
  between operations  5.46 us (4%)
  other arithmetic  2.45 us (2%)
    all_to_all x6, waiting for transfers between devices, exchange(): return lax.all_to_all(chunks, 'tp', split_axis=0, concat_axis=0, tiled=True)  40.5 us
    all_to_all x3, blocking collectives, exchange(): return lax.all_to_all(chunks, 'tp', split_axis=0, concat_axis=0, tiled=True)  34.6 us
    all_to_all x6, starting transfers between devices, exchange(): return lax.all_to_all(chunks, 'tp', split_axis=0, concat_axis=0, tiled=True)  26 us
    pallas_call x2, Pallas kernels, output_terms(): pl.pallas_call(body, out_shape=jax.ShapeDtypeStruct((shares, own, width),...  12.1 us
    pallas_call x2, Pallas kernels, attend(): call(body, (jax.ShapeDtypeStruct((shares, own, query_width + HEAD_SIZE),...  7.52 us
    pallas_call x1, Pallas kernels, first_projection(): pl.pallas_call(body, out_shape=jax.ShapeDtypeStruct((shares, own, message...  6.67 us
    pallas_call x1, Pallas kernels, next_projection(): call(body, jax.ShapeDtypeStruct((shares, own, message), bf16), [whole()]...  6.31 us
    unnamed x12, local copies, waits for them, and re-layouts  4.14 us
  transfers between devices with their start and end apart: 8, of which 6 were waited for; matrix products, arithmetic and copies ran while one was open for 3% of the time, Pallas kernels for 4%

profile of v2, /device:TPU:0, one launch (start us, length us, event | category | flops | bytes accessed | tf_op | source)
XLA Modules:
  0.0 151.9 jit_solution(5552871842432205397)
XLA Ops:
  1.3 1.3 dynamic-slice.10
  2.6 0.5 collective-permute-start
  3.1 0.7 reshape.56.s.refs_0_
  3.8 0.0 copy-start
  3.8 1.6 %copy-done = bf16[8192,128]{1,0:T(8,128)(2,1)S(1)} copy-done((bf16[8192,128]{1,0:T(8,128)(2,1)S(1)}, bf16[8192,128]{1,0:T(8,128)(2,1)}, u32[]{:S(2)}) %copy-start) | copy-done | bytes 2097176
  5.4 0.0 copy-start.4
  5.4 0.9 copy-done.4
  6.3 0.0 copy-start.5
  6.3 0.0 copy-start.2
  6.3 6.7 %shard_map.122 = bf16[8,2,640]{2,1,0:T(2,128)(2,1)} custom-call(bf16[16,8192]{1,0:T(8,128)(2,1)S(1)} %copy-done.4, bf16[1,8192]{1,0:T(2,128)(2,1)S(1)} %reshape.56.s.refs_0_, bf16[8192,512]{1,0:T(8,128)(2,1)} %wq.3, bf16[8192,128]{1,0:T(8,128)(2,1)S(1)} %copy-done), custom_call_target="tpu_custom_call" | custom-call | flops 167772160 | bytes 10485760 | tf_op jit(solution)/shard_map/pallas_call | solution.py:86
  13.0 6.8 %all-to-all-start = ((bf16[8,2,640]{2,1,0:T(2,128)(2,1)}), bf16[8,2,640]{2,1,0:T(2,128)(2,1)S(1)}, u32[]{:S(2)}, u32[]{:S(2)}) async-start(bf16[8,2,640]{2,1,0:T(2,128)(2,1)} %shard_map.122), calls=%async_computation | async-start | bytes 40960 | tf_op jit(solution)/shard_map/all_to_all | solution.py:321
  20.5 0.0 copy-done.5
  20.6 0.0 collective-permute-done
  21.1 0.8 dynamic-slice_select_fusion.1
  21.9 0.7 dynamic-slice_select_fusion.3
  22.7 0.3 collective-permute-start.1
  25.8 0.0 collective-permute-done.1
  25.8 0.6 all-to-all-done.refs_1_
  26.5 0.7 reshape.57
  27.1 5.2 %all-to-all-start.1 = ((bf16[8,16,512]{2,1,0:T(8,128)(2,1)}), bf16[8,16,512]{2,1,0:T(8,128)(2,1)S(1)}, u32[]{:S(2)}, u32[]{:S(2)}) async-start(bf16[8,16,512]{2,1,0:T(8,128)(2,1)} %reshape.57), calls=%async_computation.1 | async-start | bytes 262144 | tf_op jit(solution)/shard_map/all_to_all | solution.py:321
  32.3 0.1 fusion.1
  32.4 0.1 pad_maximum_fusion.2
  32.5 7.4 %all-to-all-done.1.refs_5_.refs_6_ = bf16[8,16,512]{2,1,0:T(8,128)(2,1)S(1)} async-done(((bf16[8,16,512]{2,1,0:T(8,128)(2,1)}), bf16[8,16,512]{2,1,0:T(8,128)(2,1)S(1)}, u32[]{:S(2)}, u32[]{:S(2)}) %all-to-all-start.1) | async-done | bytes 131104 | tf_op jit(solution)/shard_map/all_to_all | solution.py:321
  39.9 0.0 copy-done.2
  39.9 4.1 %shard_map.123 = (bf16[8,2,640]{2,1,0:T(2,128)(2,1)}, bf16[2,1024]{1,0:T(2,128)(2,1)S(1)}) custom-call(s32[2]{0:T(128)S(1)} %copy-done.5, bf16[8,2,640]{2,1,0:T(2,128)(2,1)S(1)} %all-to-all-done.refs_1_, f32[2,128]{1,0:T(2,128)S(1)} %get-tuple-element.64.refs_2_, f32[2,128]{1,0:T(2,128)S(1)} %get-tuple-element.65.refs_3_, ...), custom_call_target="tpu_custom_call" | custom-call | flops 33554432 | bytes 2097152 | tf_op jit(solution)/shard_map/pallas_call | solution.py:218
  44.0 3.3 %all-to-all-start.2 = ((bf16[8,2,640]{2,1,0:T(2,128)(2,1)}), bf16[8,2,640]{2,1,0:T(2,128)(2,1)S(1)}, u32[]{:S(2)}, u32[]{:S(2)}) async-start(bf16[8,2,640]{2,1,0:T(2,128)(2,1)} %get-tuple-element.10), calls=%async_computation.2 | async-start | bytes 40960 | tf_op jit(solution)/shard_map/all_to_all | solution.py:321
  47.3 6.5 %all-to-all-done.2.x = bf16[8,2,640]{2,1,0:T(2,128)(2,1)S(1)} async-done(((bf16[8,2,640]{2,1,0:T(2,128)(2,1)}), bf16[8,2,640]{2,1,0:T(2,128)(2,1)S(1)}, u32[]{:S(2)}, u32[]{:S(2)}) %all-to-all-start.2) | async-done | bytes 20512 | tf_op jit(solution)/shard_map/all_to_all | solution.py:321
  53.9 6.4 %shard_map.124 = f32[8,2,8192]{2,1,0:T(2,128)} custom-call(s32[1]{0:T(128)} %bitcast.mine, bf16[8,2,640]{2,1,0:T(2,128)(2,1)S(1)} %all-to-all-done.2.x, bf16[512,8192]{1,0:T(8,128)(2,1)} %wo.3, bf16[1,16,1024]{2,1,0:T(8,128)(2,1)S(1)} %slice.35.up_ref), custom_call_target="tpu_custom_call" | custom-call | flops 134217728 | bytes 8388608 | tf_op jit(solution)/shard_map/pallas_call | solution.py:259
  60.3 3.6 %all-to-all-start.3 = ((f32[8,2,8192]{2,1,0:T(2,128)}), f32[8,2,8192]{2,1,0:T(2,128)S(1)}, u32[]{:S(2)}, u32[]{:S(2)}) async-start(f32[8,2,8192]{2,1,0:T(2,128)} %shard_map.124), calls=%async_computation.3 | async-start | bytes 1048576 | tf_op jit(solution)/shard_map/all_to_all | solution.py:321
  63.9 0.9 constant_dynamic-slice_fusion.h
  64.9 11.7 %all-to-all-done.3.t = f32[8,2,8192]{2,1,0:T(2,128)S(1)} async-done(((f32[8,2,8192]{2,1,0:T(2,128)}), f32[8,2,8192]{2,1,0:T(2,128)S(1)}, u32[]{:S(2)}, u32[]{:S(2)}) %all-to-all-start.3) | async-done | bytes 524320 | tf_op jit(solution)/shard_map/all_to_all | solution.py:321
  76.6 0.3 shard_map.125
  76.9 11.6 %all_to_all.45.x = bf16[8,2,8192]{2,1,0:T(2,128)(2,1)S(1)} all-to-all(bf16[8,2,8192]{2,1,0:T(2,128)(2,1)S(1)} %get-tuple-element.11), channel_id=1, replica_groups=mesh['parts'=2,'req'=2,'tp'=8] {'tp'}, dimensions={0} | all-to-all | bytes 524288 | tf_op jit(solution)/shard_map/all_to_all | solution.py:321
  88.5 0.0 copy-done.1
  88.5 6.3 %shard_map.126 = bf16[8,2,640]{2,1,0:T(2,128)(2,1)} custom-call(bf16[8,2,8192]{2,1,0:T(2,128)(2,1)S(1)} %all_to_all.45.x, bf16[8192,512]{1,0:T(8,128)(2,1)} %wq.3, bf16[8192,128]{1,0:T(8,128)(2,1)S(1)} %copy-done.1), custom_call_target="tpu_custom_call" | custom-call | flops 167772160 | bytes 10485760 | tf_op jit(solution)/shard_map/pallas_call | solution.py:107
  94.8 3.4 %all-to-all-start.5 = ((bf16[8,2,640]{2,1,0:T(2,128)(2,1)}), bf16[8,2,640]{2,1,0:T(2,128)(2,1)S(1)}, u32[]{:S(2)}, u32[]{:S(2)}) async-start(bf16[8,2,640]{2,1,0:T(2,128)(2,1)} %shard_map.126), calls=%async_computation.5 | async-start | bytes 40960 | tf_op jit(solution)/shard_map/all_to_all | solution.py:321
  98.3 0.1 pad_maximum_fusion.4
  98.3 6.5 %all-to-all-done.5.refs_1_ = bf16[8,2,640]{2,1,0:T(2,128)(2,1)S(1)} async-done(((bf16[8,2,640]{2,1,0:T(2,128)(2,1)}), bf16[8,2,640]{2,1,0:T(2,128)(2,1)S(1)}, u32[]{:S(2)}, u32[]{:S(2)}) %all-to-all-start.5) | async-done | bytes 20512 | tf_op jit(solution)/shard_map/all_to_all | solution.py:321
  104.9 1.6 %copy-done.3 = bf16[2,512,1024]{2,1,0:T(8,128)(2,1)S(1)} copy-done((bf16[2,512,1024]{2,1,0:T(8,128)(2,1)S(1)}, bf16[2,512,1024]{2,1,0:T(8,128)(2,1)}, u32[]{:S(2)}) %copy-start.3) | copy-done | bytes 2097176
  106.5 3.5 %shard_map.127 = (bf16[8,2,640]{2,1,0:T(2,128)(2,1)S(1)}, bf16[2,1024]{1,0:T(2,128)(2,1)S(1)}) custom-call(s32[2]{0:T(128)S(1)} %copy-done.5, bf16[8,2,640]{2,1,0:T(2,128)(2,1)S(1)} %all-to-all-done.5.refs_1_, bf16[2,1024]{1,0:T(2,128)(2,1)S(1)} %get-tuple-element.12.refs_2_, f32[2,128]{1,0:T(2,128)S(1)} %get-tuple-element.66.refs_3_, ...), custom_call_target="tpu_custom_call" | custom-call | flops 33554432 | bytes 2097152 | tf_op jit(solution)/shard_map/pallas_call | solution.py:218
  109.9 9.0 %all_to_all.46.x = bf16[8,2,640]{2,1,0:T(2,128)(2,1)S(1)} all-to-all(bf16[8,2,640]{2,1,0:T(2,128)(2,1)S(1)} %get-tuple-element.13), channel_id=1, replica_groups=mesh['parts'=2,'req'=2,'tp'=8] {'tp'}, dimensions={0} | all-to-all | bytes 40960 | tf_op jit(solution)/shard_map/all_to_all | solution.py:321
  118.9 5.6 %shard_map.128 = f32[8,2,8192]{2,1,0:T(2,128)S(1)} custom-call(s32[1]{0:T(128)} %bitcast.mine, bf16[8,2,640]{2,1,0:T(2,128)(2,1)S(1)} %all_to_all.46.x, bf16[512,8192]{1,0:T(8,128)(2,1)} %wo.3, bf16[1,16,1024]{2,1,0:T(8,128)(2,1)S(1)} %slice.35.up_ref), custom_call_target="tpu_custom_call" | custom-call | flops 134217728 | bytes 8388608 | tf_op jit(solution)/shard_map/pallas_call | solution.py:259
  124.5 14.0 %all_to_all.47.t = f32[8,2,8192]{2,1,0:T(2,128)S(1)} all-to-all(f32[8,2,8192]{2,1,0:T(2,128)S(1)} %shard_map.128), channel_id=1, replica_groups=mesh['parts'=2,'req'=2,'tp'=8] {'tp'}, dimensions={0} | all-to-all | bytes 1048576 | tf_op jit(solution)/shard_map/all_to_all | solution.py:321
  138.5 0.8 shard_map.129
  139.2 3.6 %all-to-all-start.8 = ((bf16[8,2,8192]{2,1,0:T(2,128)(2,1)}), bf16[8,2,8192]{2,1,0:T(2,128)(2,1)S(1)}, u32[]{:S(2)}, u32[]{:S(2)}) async-start(bf16[8,2,8192]{2,1,0:T(2,128)(2,1)} %shard_map.129), calls=%async_computation.8 | async-start | bytes 524288 | tf_op jit(solution)/shard_map/all_to_all | solution.py:321
  142.9 0.6 pad_maximum_fusion.1
  143.5 7.6 %all-to-all-done.8 = bf16[8,2,8192]{2,1,0:T(2,128)(2,1)S(1)} async-done(((bf16[8,2,8192]{2,1,0:T(2,128)(2,1)}), bf16[8,2,8192]{2,1,0:T(2,128)(2,1)S(1)}, u32[]{:S(2)}, u32[]{:S(2)}) %all-to-all-start.8) | async-done | bytes 262176 | tf_op jit(solution)/shard_map/all_to_all | solution.py:321
  151.1 0.8 reshape.58
  (8 shorter events, 0.0 us)
Async XLA Ops:
  2.6 18.0 %collective-permute-start = (s32[1]{0:T(128)}, s32[1]{0:T(128)}, u32[]{:S(2)}, u32[]{:S(2)}) collective-permute-start(s32[1]{0:T(128)} %dynamic-slice.10), channel_id=1, source_target_pairs={{0,8},{8,0},{1,9},{9,1},{2,10},{10,2},{3,11},{11,3},{4,12},{12,4},... | collective-permute-start | bytes 20 | tf_op jit(solution)/shard_map/ppermute | solution.py:309
  3.8 1.6 %copy-start = (bf16[8192,128]{1,0:T(8,128)(2,1)S(1)}, bf16[8192,128]{1,0:T(8,128)(2,1)}, u32[]{:S(2)}) copy-start(bf16[8192,128]{1,0:T(8,128)(2,1)} %wp.3) | copy-start | bytes 6291460
  5.4 0.9 copy-start.4
  6.3 14.2 %copy-start.5 = (s32[2]{0:T(128)S(1)}, s32[2]{0:T(128)}, u32[]{:S(2)}) copy-start(s32[2]{0:T(128)} %refs_0_.3) | copy-start | bytes 28
  6.3 33.6 %copy-start.2 = (bf16[2,512,1024]{2,1,0:T(8,128)(2,1)S(1)}, bf16[2,512,1024]{2,1,0:T(8,128)(2,1)}, u32[]{:S(2)}) copy-start(bf16[2,512,1024]{2,1,0:T(8,128)(2,1)} %refs_5_.1) | copy-start | bytes 6291460
  13.0 13.4 %all-to-all-start = ((bf16[8,2,640]{2,1,0:T(2,128)(2,1)}), bf16[8,2,640]{2,1,0:T(2,128)(2,1)S(1)}, u32[]{:S(2)}, u32[]{:S(2)}) async-start(bf16[8,2,640]{2,1,0:T(2,128)(2,1)} %shard_map.122), calls=%async_computation | async-start | bytes 40960 | tf_op jit(solution)/shard_map/all_to_all | solution.py:321
  22.7 3.1 %collective-permute-start.1 = (bf16[1,16,1536]{2,1,0:T(8,128)(2,1)S(1)}, bf16[1,16,1536]{2,1,0:T(8,128)(2,1)S(1)}, u32[]{:S(2)}, u32[]{:S(2)}) collective-permute-start(bf16[1,16,1536]{2,1,0:T(8,128)(2,1)S(1)} %pad_maximum_fusion), channel_id=1, source_target_pairs={{0,8},{8,0},{1,9},{9,1},{2,10},{10,2},{3,11},{11,3},{4,12},{12,4},... | collective-permute-start | bytes 147464 | tf_op jit(solution)/shard_map/ppermute | solution.py:315
  27.1 12.8 %all-to-all-start.1 = ((bf16[8,16,512]{2,1,0:T(8,128)(2,1)}), bf16[8,16,512]{2,1,0:T(8,128)(2,1)S(1)}, u32[]{:S(2)}, u32[]{:S(2)}) async-start(bf16[8,16,512]{2,1,0:T(8,128)(2,1)} %reshape.57), calls=%async_computation.1 | async-start | bytes 262144 | tf_op jit(solution)/shard_map/all_to_all | solution.py:321
  44.0 9.9 %all-to-all-start.2 = ((bf16[8,2,640]{2,1,0:T(2,128)(2,1)}), bf16[8,2,640]{2,1,0:T(2,128)(2,1)S(1)}, u32[]{:S(2)}, u32[]{:S(2)}) async-start(bf16[8,2,640]{2,1,0:T(2,128)(2,1)} %get-tuple-element.10), calls=%async_computation.2 | async-start | bytes 40960 | tf_op jit(solution)/shard_map/all_to_all | solution.py:321
  60.3 28.2 %copy-start.1 = (bf16[8192,128]{1,0:T(8,128)(2,1)S(1)}, bf16[8192,128]{1,0:T(8,128)(2,1)}, u32[]{:S(2)}) copy-start(bf16[8192,128]{1,0:T(8,128)(2,1)} %wp.3) | copy-start | bytes 6291460
  60.3 16.3 %all-to-all-start.3 = ((f32[8,2,8192]{2,1,0:T(2,128)}), f32[8,2,8192]{2,1,0:T(2,128)S(1)}, u32[]{:S(2)}, u32[]{:S(2)}) async-start(f32[8,2,8192]{2,1,0:T(2,128)} %shard_map.124), calls=%async_computation.3 | async-start | bytes 1048576 | tf_op jit(solution)/shard_map/all_to_all | solution.py:321
  94.8 10.0 %all-to-all-start.5 = ((bf16[8,2,640]{2,1,0:T(2,128)(2,1)}), bf16[8,2,640]{2,1,0:T(2,128)(2,1)S(1)}, u32[]{:S(2)}, u32[]{:S(2)}) async-start(bf16[8,2,640]{2,1,0:T(2,128)(2,1)} %shard_map.126), calls=%async_computation.5 | async-start | bytes 40960 | tf_op jit(solution)/shard_map/all_to_all | solution.py:321
  104.9 1.6 %copy-start.3 = (bf16[2,512,1024]{2,1,0:T(8,128)(2,1)S(1)}, bf16[2,512,1024]{2,1,0:T(8,128)(2,1)}, u32[]{:S(2)}) copy-start(bf16[2,512,1024]{2,1,0:T(8,128)(2,1)} %refs_5_.1) | copy-start | bytes 6291460
  139.2 11.9 %all-to-all-start.8 = ((bf16[8,2,8192]{2,1,0:T(2,128)(2,1)}), bf16[8,2,8192]{2,1,0:T(2,128)(2,1)S(1)}, u32[]{:S(2)}, u32[]{:S(2)}) async-start(bf16[8,2,8192]{2,1,0:T(2,128)(2,1)} %shard_map.129), calls=%async_computation.8 | async-start | bytes 524288 | tf_op jit(solution)/shard_map/all_to_all | solution.py:321

commit v3 on v2

--- a/solution.py
+++ b/solution.py
@@ -16,7 +16,7 @@
 
 rope_base = 500000.0
 norm_epsilon = 1e-05
-term_type = jnp.float32
+term_type = jnp.bfloat16
 f32 = jnp.float32
 bf16 = jnp.bfloat16
 MIB = 1 << 20
@@ -26,7 +26,7 @@
     return pl.BlockSpec(memory_space=kind)
 
 
-def call(body, outs, ins, flops, data_bytes, limit=48):
+def call(body, outs, ins, flops, data_bytes, limit=16):
     return pl.pallas_call(
         body,
         out_shape=outs,
@@ -37,83 +37,176 @@
     )
 
 
+def far(array):
+    return pltpu.with_memory_space_constraint(array, pltpu.HBM)
+
+
 def rows_of(ref, start, width):
     pieces = [ref[j, :, pl.ds(start, width)].astype(f32) for j in range(ref.shape[0])]
     return jnp.concatenate(pieces, axis=0).astype(bf16)
 
 
-def project(source, query_weight, pair_weight, chunk_of, shares):
-    depth, query_width = query_weight.shape
-    pair_width = pair_weight.shape[1]
-    step = 512
+def streamed(weights, kept, sems, step, axis):
+    def copies(i):
+        piece = pl.ds(pl.multiple_of(i * step, step), step)
+        at = (piece, slice(None)) if axis == 0 else (slice(None), piece)
+        return [
+            pltpu.make_async_copy(w.at[at], k.at[at], sems.at[n, i])
+            for n, (w, k) in enumerate(zip(weights, kept))
+        ]
+
+    return copies
+
+
+def project(weights, chunk_of, rows, step, copies):
+    depth = weights[0].shape[0]
 
     def loop(i, sums):
         at = pl.multiple_of(i * step, step)
+        for copy in copies(i):
+            copy.wait()
         part = chunk_of(at, step)
-        rows = pl.ds(at, step)
-        return (
-            sums[0] + jnp.dot(part, query_weight[rows, :], preferred_element_type=f32),
-            sums[1] + jnp.dot(part, pair_weight[rows, :], preferred_element_type=f32),
+        return tuple(
+            total + jnp.dot(part, w[pl.ds(at, step), :], preferred_element_type=f32)
+            for total, w in zip(sums, weights)
         )
 
-    count = shares[0] * shares[1]
-    zero = (jnp.zeros((count, query_width), f32), jnp.zeros((count, pair_width), f32))
-    return lax.fori_loop(0, depth // step, loop, zero, unroll=2)
+    zero = tuple(jnp.zeros((rows, w.shape[1]), f32) for w in weights)
+    return lax.fori_loop(0, depth // step, loop, zero)
 
 
 def store_shares(out, query, pair):
     shares, own, _ = out.shape
     width = query.shape[1]
     for j in range(shares):
-        out[j, :, :width] = query[j * own : (j + 1) * own].astype(bf16)
-        out[j, :, width:] = pair[j * own : (j + 1) * own].astype(bf16)
-
-
-def first_projection(hidden, scale, query_weight, pair_weight, own):
-    rows, width = hidden.shape
-    shares = rows // own
-
-    def body(h, s, wq, wp, out, normed):
-        wide = h[...].astype(f32)
-        mean = jnp.mean(wide * wide, axis=-1, keepdims=True)
-        normed[...] = (wide * lax.rsqrt(mean + norm_epsilon) * s[...].astype(f32)).astype(bf16)
-        sums = project(
-            h, wq, wp, lambda at, n: normed[:, pl.ds(at, n)], (shares, own)
-        )
+        lines = slice(j * own, (j + 1) * own)
+        out[j, :, :width] = query[lines].astype(bf16)
+        out[j, :, width:] = pair[lines].astype(bf16)
+
+
+def projection(source, weights, own, scale=None):
+    width = weights[0].shape[0]
+    shares = lax.axis_size("tp")
+    rows = shares * own
+    message = sum(w.shape[1] for w in weights)
+    step = 1024
+    parts = width // step
+    first = scale is not None
+
+    def body(*refs):
+        if first:
+            source_ref, s, wq, wp, out, kept_q, kept_p, sems, x, gains, normed, pre = refs
+            loads = [
+                pltpu.make_async_copy(source_ref, x, pre.at[0]),
+                pltpu.make_async_copy(s, gains, pre.at[1]),
+            ]
+            for load in loads:
+                load.start()
+        else:
+            x, wq, wp, out, kept_q, kept_p, sems = refs
+        copies = streamed((wq, wp), (kept_q, kept_p), sems, step, 0)
+        for i in range(parts):
+            for copy in copies(i):
+                copy.start()
+        if first:
+            for load in loads:
+                load.wait()
+            wide = x[...].astype(f32)
+            ratio = lax.rsqrt(jnp.mean(wide * wide, axis=-1, keepdims=True) + norm_epsilon)
+            gain = gains[...].astype(f32)
+            for c in range(width // HEAD_SIZE):
+                columns = slice(c * HEAD_SIZE, (c + 1) * HEAD_SIZE)
+                normed[:, columns] = (
+                    x[:, columns].astype(f32) * ratio * gain[c : c + 1, :]
+                ).astype(bf16)
+            chunk_of = lambda at, n: normed[:, pl.ds(at, n)]
+        else:
+            chunk_of = lambda at, n: rows_of(x, at, n)
+        sums = project((kept_q, kept_p), chunk_of, rows, step, copies)
         store_shares(out, *sums)
 
-    message = query_weight.shape[1] + pair_weight.shape[1]
+    scratch = [pltpu.VMEM(w.shape, bf16) for w in weights]
+    scratch.append(pltpu.SemaphoreType.DMA((2, parts)))
+    operands = [source, *map(far, weights)]
+    specs = [whole(), whole(pltpu.HBM), whole(pltpu.HBM)]
+    if first:
+        operands[:1] = [far(source), far(scale)]
+        specs[:1] = [whole(pltpu.HBM)] * 2
+        scratch += [
+            pltpu.VMEM(source.shape, bf16),
+            pltpu.VMEM(scale.shape, bf16),
+            pltpu.VMEM(source.shape, bf16),
+            pltpu.SemaphoreType.DMA((2,)),
+        ]
     return pl.pallas_call(
         body,
         out_shape=jax.ShapeDtypeStruct((shares, own, message), bf16),
-        in_specs=[whole()] * 4,
+        in_specs=specs,
         out_specs=whole(),
-        scratch_shapes=[pltpu.VMEM((rows, width), bf16)],
-        compiler_params=pltpu.CompilerParams(vmem_limit_bytes=48 * MIB),
+        scratch_shapes=scratch,
+        compiler_params=pltpu.CompilerParams(vmem_limit_bytes=24 * MIB),
         cost_estimate=pl.CostEstimate(
-            flops=2 * rows * width * message, bytes_accessed=2 * width * message, transcendentals=0
+            flops=2 * rows * width * message,
+            bytes_accessed=2 * width * message,
+            transcendentals=0,
         ),
-    )(hidden, scale, query_weight, pair_weight)
-
-
-def next_projection(normed, query_weight, pair_weight):
-    shares, own, width = normed.shape
-
-    def body(x, wq, wp, out):
-        sums = project(x, wq, wp, lambda at, n: rows_of(x, at, n), (shares, own))
-        store_shares(out, *sums)
-
-    message = query_weight.shape[1] + pair_weight.shape[1]
-    return call(
+    )(*operands)
+
+
+def fetch(block, per_block, slots, side, here, other, target, sem):
+    stored_here = here.shape[0]
+    slot = slots[per_block[block]]
+    at = lax.rem(slot, jnp.int32(stored_here))
+    mine = lax.div(slot, jnp.int32(stored_here)) == side[0]
+
+    @pl.when(mine)
+    def _():
+        pltpu.make_async_copy(here.at[at], target.at[block], sem.at[block]).start()
+
+    @pl.when(jnp.logical_not(mine))
+    def _():
+        pltpu.make_async_copy(other.at[at], target.at[block], sem.at[block]).start()
+
+    return pltpu.make_async_copy(here.at[0], target.at[block], sem.at[block])
+
+
+def add_down(message, adapters, here, other, blocks):
+    shares, own, width = message.shape
+    rank, columns = here.shape[1:]
+    lead = rank // own * columns
+
+    def body(per_block, slots, side, m, here_ref, other_ref, out, piece, sem):
+        waits = [
+            fetch(b, per_block, slots, side, here_ref, other_ref, piece, sem)
+            for b in range(blocks)
+        ]
+        for j in range(shares):
+            out[j, :, lead:] = m[j]
+        for wait in waits:
+            wait.wait()
+        for b in range(blocks):
+            lines = [
+                piece[b, m * own : (m + 1) * own, :].astype(f32) for m in range(rank // own)
+            ]
+            packed = jnp.concatenate(lines, axis=1).astype(bf16)
+            for j in range(b * BLOCK // own, (b + 1) * BLOCK // own):
+                out[j, :, :lead] = packed
+
+    smem = whole(pltpu.SMEM)
+    return pl.pallas_call(
         body,
-        jax.ShapeDtypeStruct((shares, own, message), bf16),
-        [whole()] * 3,
-        2 * shares * own * width * message,
-        2 * width * message,
-    )(normed, query_weight, pair_weight)
-
-
-def attend(arrived, pairs, older, angles, lengths, cache, down, step):
+        out_shape=jax.ShapeDtypeStruct((shares, own, lead + width), bf16),
+        in_specs=[smem, smem, smem, whole(), whole(pltpu.HBM), whole(pltpu.HBM)],
+        out_specs=whole(),
+        scratch_shapes=[
+            pltpu.VMEM((blocks, rank, columns), bf16),
+            pltpu.SemaphoreType.DMA((blocks,)),
+        ],
+        compiler_params=pltpu.CompilerParams(vmem_limit_bytes=16 * MIB),
+    )(*adapters, message, far(here), far(other))
+
+
+def attend(arrived, pairs, older, angles, lengths, cache, down, step, lead, rank):
     shares, own, message = arrived.shape
     context, width = cache.shape[1:]
     half = width // 2
@@ -121,16 +214,25 @@
     per_share = query_width // HEAD_SIZE
     groups = QUERY_HEAD_COUNT // KV_HEADS
     pair_inside = pairs is None
-    rank = down.shape[1]
 
     def body(*refs):
         refs = list(refs)
         lens, x = refs.pop(0), refs.pop(0)
         pair_ref = None if pair_inside else refs.pop(0)
         old = refs.pop(0) if step else None
-        cos_ref, sin_ref, kv, down_ref, out, new = refs
+        cos_ref, sin_ref, kv = refs[:3]
+        if step:
+            down_ref, out, new = refs[3:]
+        else:
+            out, new, down_ref = refs[3:]
+            for j in range(shares):
+                lines = [
+                    x[j, :, m * query_width : (m + 1) * query_width].astype(f32)
+                    for m in range(rank // own)
+                ]
+                down_ref[j] = jnp.concatenate(lines, axis=0).astype(bf16)
         place = lax.broadcasted_iota(jnp.int32, (groups, context), 1)
-        rows = [x[j].astype(f32) for j in range(shares)]
+        rows = [x[j, :, lead:].astype(f32) for j in range(shares)]
         outputs = []
         fresh = []
         for r in range(own):
@@ -213,62 +315,93 @@
     for extra in ([] if pair_inside else [pairs]) + ([older] if step else []):
         operands.append(extra)
         specs.append(whole())
-    operands += [angles[0], angles[1], cache, down]
-    specs += [whole()] * 4
-    return call(
+    operands += [angles[0], angles[1], cache] + ([down] if step else [])
+    specs += [whole()] * (4 if step else 3)
+    outs = [
+        jax.ShapeDtypeStruct((shares, own, query_width + HEAD_SIZE), bf16),
+        jax.ShapeDtypeStruct((own, width), bf16),
+    ]
+    if not step:
+        outs.append(jax.ShapeDtypeStruct((shares, rank, query_width), bf16))
+    return pl.pallas_call(
         body,
-        (
-            jax.ShapeDtypeStruct((shares, own, query_width + HEAD_SIZE), bf16),
-            jax.ShapeDtypeStruct((own, width), bf16),
+        out_shape=tuple(outs),
+        in_specs=specs,
+        out_specs=(whole(),) * len(outs),
+        compiler_params=pltpu.CompilerParams(vmem_limit_bytes=16 * MIB),
+        cost_estimate=pl.CostEstimate(
+            flops=8 * own * QUERY_HEAD_COUNT * HEAD_SIZE * context,
+            bytes_accessed=2 * own * context * width,
+            transcendentals=0,
         ),
-        specs,
-        8 * own * QUERY_HEAD_COUNT * HEAD_SIZE * context,
-        2 * own * context * width,
     )(*operands)
 
 
-def output_terms(arrived, output_weight, up, blocks):
+def output_terms(arrived, output_weight, adapters, here, other, blocks):
     shares, own, _ = arrived.shape
     query_width, width = output_weight.shape
-    share_width = up.shape[2]
-    rank = up.shape[1]
+    rank, share_width = here.shape[1:]
     rows = shares * own
     step = 1024
-
-    def body(mine, x, wo, up_ref, out, total):
+    parts = width // step
+
+    def body(mine, per_block, slots, side, x, wo, here_ref, other_ref, *refs):
+        out, total, kept, up, sem, sems = refs
+        copies = streamed((wo,), (kept,), sems, step, 1)
+        for i in range(parts):
+            copies(i)[0].start()
+        waits = [
+            fetch(b, per_block, slots, side, here_ref, other_ref, up, sem) for b in range(blocks)
+        ]
         heads = rows_of(x, 0, query_width)
         low = rows_of(x, query_width, HEAD_SIZE)[:, :rank]
 
         def loop(i, carry):
             at = pl.multiple_of(i * step, step)
+            copies(i)[0].wait()
             total[:, pl.ds(at, step)] = jnp.dot(
-                heads, wo[:, pl.ds(at, step)], preferred_element_type=f32
+                heads, kept[:, pl.ds(at, step)], preferred_element_type=f32
             )
             return carry
 
-        lax.fori_loop(0, width // step, loop, 0)
+        lax.fori_loop(0, parts, loop, 0)
         start = pl.multiple_of(mine[0] * share_width, share_width)
         for b in range(blocks):
+            waits[b].wait()
             lines = slice(b * BLOCK, (b + 1) * BLOCK)
             total[lines, pl.ds(start, share_width)] += jnp.dot(
-                low[lines], up_ref[b], preferred_element_type=f32
+                low[lines], up[b], preferred_element_type=f32
             )
         for j in range(shares):
             out[j] = total[j * own : (j + 1) * own, :].astype(out.dtype)
 
+    smem, hbm = whole(pltpu.SMEM), whole(pltpu.HBM)
     return pl.pallas_call(
         body,
         out_shape=jax.ShapeDtypeStruct((shares, own, width), term_type),
-        in_specs=[whole(pltpu.SMEM)] + [whole()] * 3,
+        in_specs=[smem] * 4 + [whole(), hbm, hbm, hbm],
         out_specs=whole(),
-        scratch_shapes=[pltpu.VMEM((rows, width), f32)],
-        compiler_params=pltpu.CompilerParams(vmem_limit_bytes=48 * MIB),
+        scratch_shapes=[
+            pltpu.VMEM((rows, width), f32),
+            pltpu.VMEM(output_weight.shape, bf16),
+            pltpu.VMEM((blocks, rank, share_width), bf16),
+            pltpu.SemaphoreType.DMA((blocks,)),
+            pltpu.SemaphoreType.DMA((1, parts)),
+        ],
+        compiler_params=pltpu.CompilerParams(vmem_limit_bytes=24 * MIB),
         cost_estimate=pl.CostEstimate(
             flops=2 * rows * width * query_width,
             bytes_accessed=2 * width * query_width,
             transcendentals=0,
         ),
-    )(lax.axis_index("tp").astype(jnp.int32).reshape(1), arrived, output_weight, up)
+    )(
+        lax.axis_index("tp").astype(jnp.int32).reshape(1),
+        *adapters,
+        arrived,
+        far(output_weight),
+        far(here),
+        far(other),
+    )
 
 
 def close_step(terms, hidden, scale):
@@ -286,7 +419,15 @@
             kept[...] = rounded
             wide = rounded.astype(f32)
             mean = jnp.mean(wide * wide, axis=-1, keepdims=True)
-            spread = (wide * lax.rsqrt(mean + norm_epsilon) * s[...].astype(f32)).astype(bf16)
+            wide = wide * lax.rsqrt(mean + norm_epsilon)
+            gain = s[...].astype(f32)
+            spread = jnp.concatenate(
+                [
+                    wide[:, c * HEAD_SIZE : (c + 1) * HEAD_SIZE] * gain[c : c + 1, :]
+                    for c in range(width // HEAD_SIZE)
+                ],
+                axis=1,
+            ).astype(bf16)
         else:
             (out,) = refs
         for j in range(shares):
@@ -300,21 +441,6 @@
     return call(
         body, tuple(outs), [whole()] * len(operands), 8 * own * width, 6 * shares * own * width
     )(*operands)
-
-
-def block_adapters(adapter_per_block, adapter_storage_slot, down, up):
-    own = lax.axis_index("req")
-    stored_here = down.shape[0]
-    slot = adapter_storage_slot[adapter_per_block]
-    other_slot = lax.ppermute(slot, "req", [(0, 1), (1, 0)])
-
-    def piece(which):
-        at = jnp.clip(which - own * stored_here, 0, stored_here - 1)
-        return jnp.concatenate([jnp.take(down, at, axis=0), jnp.take(up, at, axis=0)], axis=2)
-
-    sent = lax.ppermute(piece(other_slot), "req", [(0, 1), (1, 0)])
-    held = jnp.where((slot // stored_here == own)[:, None, None], piece(slot), sent)
-    return held[:, :, : down.shape[2]], held[:, :, down.shape[2] :]
 
 
 def exchange(chunks):
@@ -341,17 +467,25 @@
     blocks = rows_req // BLOCK
     width = input_hidden_rows.shape[1]
     query_width = query_weight.shape[1]
-    scale = input_norm_scale.reshape(1, width)
-    down, up = block_adapters(
-        adapter_per_block, adapter_storage_slot, adapter_down_projection, adapter_up_projection
+    rank = adapter_down_projection.shape[1]
+    scale = input_norm_scale.reshape(width // HEAD_SIZE, HEAD_SIZE)
+    adapters = (
+        adapter_per_block,
+        adapter_storage_slot,
+        lax.axis_index("req").astype(jnp.int32).reshape(1),
     )
-    down_chunks = jnp.repeat(down, tp_count // blocks, axis=0)
-    down_own = exchange(down_chunks)
+    cores = [(0, 1), (1, 0)]
+    other_down = lax.ppermute(adapter_down_projection, "req", cores)
+    other_up = lax.ppermute(adapter_up_projection, "req", cores)
+    lead = rank // own * query_width
     half_head = HEAD_SIZE // 2
     frequency = rope_base ** (-(jnp.arange(half_head, dtype=f32) * 2.0 / HEAD_SIZE))
     hidden = lax.dynamic_slice_in_dim(input_hidden_rows, tp_index * own, own, 0)
     stored = []
-    message = first_projection(input_hidden_rows, scale, query_weight, key_value_weight, own)
+    weights = (query_weight, key_value_weight)
+    message = projection(input_hidden_rows, weights, own, scale)
+    message = add_down(message, adapters, adapter_down_projection, other_down, blocks)
+    down = None
     for step in range(STEPS):
         angle = (lengths + step).astype(f32)[:, None] * frequency[None, :]
         cosine, sine = jnp.cos(angle), jnp.sin(angle)
@@ -360,17 +494,33 @@
             jnp.concatenate([-sine, sine], axis=1),
         )
         arrived = exchange(message)
+        start = 0 if step else lead
         pairs = None
         if key_value_weight.shape[1] != HEAD_SIZE:
-            pairs = arrived[:, :, query_width:].transpose(1, 0, 2).reshape(own, -1)
-        attended, fresh = attend(
-            arrived, pairs, stored[-1] if step else None, angles, lengths, cache, down_own, step
+            pairs = arrived[:, :, start + query_width :].transpose(1, 0, 2).reshape(own, -1)
+        attended, fresh, *first = attend(
+            arrived,
+            pairs,
+            stored[-1] if step else None,
+            angles,
+            lengths,
+            cache,
+            down,
+            step,
+            start,
+            rank,
         )
         stored.append(fresh)
-        terms = exchange(output_terms(exchange(attended), output_weight, up, blocks))
+        if not step:
+            (down,) = first
+        terms = exchange(
+            output_terms(
+                exchange(attended), output_weight, adapters, adapter_up_projection, other_up, blocks
+            )
+        )
         if step < STEPS - 1:
             spread, hidden = close_step(terms, hidden, scale)
-            message = next_projection(exchange(spread), query_weight, key_value_weight)
+            message = projection(exchange(spread), weights, own)
         else:
             (spread,) = close_step(terms, hidden, None)
     return (exchange(spread).reshape(rows_req, width), jnp.stack(stored, axis=0))

time: 153 us -> 124 us (0.81)
  local copies, waits for them, and re-layouts: 8.61 us -> 1.77 us
  starting transfers between devices: 26.8 us -> 21.4 us
  waiting for transfers between devices: 40.5 us -> 35.1 us
  blocking collectives: 34.6 us -> 30.5 us
  between operations: 5.46 us -> 1.44 us
  Pallas kernels: 33.6 us -> 31.8 us
  other arithmetic: 2.45 us -> 0.9 us
    all_to_all x6 -> x5, waiting for transfers between devices: 40.5 us -> 35.1 us  [exchange(): return lax.all_to_all(chunks, 'tp', split_axis=0, concat_axis=0, tiled=True)]
    all_to_all x6 -> x5, starting transfers between devices: 26 us -> 20.8 us  [exchange(): return lax.all_to_all(chunks, 'tp', split_axis=0, concat_axis=0, tiled=True)]
    unnamed x12 -> x8, local copies, waits for them, and re-layouts: 4.14 us -> 0.02 us
    all_to_all x3, blocking collectives: 34.6 us -> 30.5 us  [exchange(): return lax.all_to_all(chunks, 'tp', split_axis=0, concat_axis=0, tiled=True)]
    pallas_call x2, Pallas kernels: 12.1 us -> 9.8 us  [output_terms(): pl.pallas_call(body, out_shape=jax.ShapeDtypeStruct((shares, own, width),...]
    select_n x3 -> x0, other arithmetic: 1.55 us -> none  [the longest x1 0.79 us: piece(): jnp.take(up, at, axis=0)]
    pallas_call x4 -> x5, Pallas kernels: 20.5 us -> 21 us  [the longest x2 11.5 us: projection(): pl.pallas_call(body, out_shape=jax.ShapeDtypeStruct((shares, own, message...]
  transfers between devices with their start and end apart: 8 -> 7, of which waited for: 6 -> 5; matrix products, arithmetic and copies ran while one was open for 3% -> 2% of each run, Pallas kernels for 4% -> 10%
where the time goes in v3:
time: 124 us; the launch traced here: 123 us
  waiting for transfers between devices  35.1 us (28%)
  Pallas kernels  31.8 us (26%)
  blocking collectives  30.5 us (25%)
  starting transfers between devices  21.4 us (17%)
  local copies, waits for them, and re-layouts  1.77 us (1%)
  between operations  1.44 us (1%)
    all_to_all x5, waiting for transfers between devices, exchange(): return lax.all_to_all(chunks, 'tp', split_axis=0, concat_axis=0, tiled=True)  35.1 us
    all_to_all x3, blocking collectives, exchange(): return lax.all_to_all(chunks, 'tp', split_axis=0, concat_axis=0, tiled=True)  30.5 us
    all_to_all x5, starting transfers between devices, exchange(): return lax.all_to_all(chunks, 'tp', split_axis=0, concat_axis=0, tiled=True)  20.8 us
    pallas_call x2, Pallas kernels, projection(): pl.pallas_call(body, out_shape=jax.ShapeDtypeStruct((shares, own, message...  11.5 us
    pallas_call x2, Pallas kernels, output_terms(): pl.pallas_call(body, out_shape=jax.ShapeDtypeStruct((shares, own, width),...  9.8 us
    pallas_call x2, Pallas kernels, attend(): pl.pallas_call(body, out_shape=tuple(outs), in_specs=specs, out_specs=(wh...  7.52 us
  transfers between devices with their start and end apart: 7, of which 5 were waited for; matrix products, arithmetic and copies ran while one was open for 2% of the time, Pallas kernels for 10%

profile of v3, /device:TPU:0, one launch (start us, length us, event | category | flops | bytes accessed | tf_op | source)
XLA Modules:
  0.0 122.9 jit_solution(17572582939051057541)
XLA Ops:
  0.6 0.5 collective-permute-start.1
  1.1 0.1 collective-permute-start
  1.9 0.0 copy-start.3
  1.9 0.0 copy-start.2
  1.9 6.5 %shard_map.122.m = bf16[8,2,640]{2,1,0:T(2,128)(2,1)S(1)} custom-call(bf16[16,8192]{1,0:T(8,128)(2,1)} %refs_0_.3, bf16[64,128]{1,0:T(8,128)(2,1)} %bitcast.5, bf16[8192,512]{1,0:T(8,128)(2,1)} %refs_1_.1, bf16[8192,128]{1,0:T(8,128)(2,1)} %refs_2_.3), custom_call_target="tpu_custom_call" | custom-call | flops 167772160 | bytes 10485760 | tf_op jit(solution)/shard_map/pallas_call | solution.py:141
  8.4 0.0 copy-start
  8.4 0.0 copy-done.3
  8.5 0.0 collective-permute-done.other_ref
  8.5 0.0 copy-done.2
  8.5 2.0 %shard_map.123 = bf16[8,2,4736]{2,1,0:T(2,128)(2,1)} custom-call(s32[1]{0:T(128)S(6)} %copy.13.per_block, s32[128]{0:T(128)S(1)} %copy-done.2, s32[1]{0:T(128)} %bitcast.1.side, bf16[8,2,640]{2,1,0:T(2,128)(2,1)S(1)} %shard_map.122.m, bf16[64,16,512]{2,1,0:T(8,128)(2,1)} %here_ref.3, bf16[64,16,512]{2,1,0:T(8,128)(2,1)} %collective-permute-done.other_ref), custom_call_target="tpu_custom_call" | custom-call | tf_op jit(solution)/shard_map/pallas_call | solution.py:196
  10.5 7.3 %all-to-all-start = ((bf16[8,2,4736]{2,1,0:T(2,128)(2,1)}), bf16[8,2,4736]{2,1,0:T(2,128)(2,1)S(1)}, u32[]{:S(2)}, u32[]{:S(2)}) async-start(bf16[8,2,4736]{2,1,0:T(2,128)(2,1)} %shard_map.123), calls=%async_computation | async-start | bytes 303104 | tf_op jit(solution)/shard_map/all_to_all | solution.py:447
  17.8 0.1 fusion.1
  17.9 0.1 pad_maximum_fusion.1
  18.0 7.3 %all-to-all-done.refs_1_ = bf16[8,2,4736]{2,1,0:T(2,128)(2,1)S(1)} async-done(((bf16[8,2,4736]{2,1,0:T(2,128)(2,1)}), bf16[8,2,4736]{2,1,0:T(2,128)(2,1)S(1)}, u32[]{:S(2)}, u32[]{:S(2)}) %all-to-all-start) | async-done | bytes 151584 | tf_op jit(solution)/shard_map/all_to_all | solution.py:447
  25.3 0.0 copy-done
  25.3 4.1 %shard_map.124 = (bf16[8,2,640]{2,1,0:T(2,128)(2,1)}, bf16[2,1024]{1,0:T(2,128)(2,1)S(1)}, bf16[8,16,512]{2,1,0:T(8,128)(2,1)S(1)}) custom-call(s32[2]{0:T(128)S(1)} %copy-done.3, bf16[8,2,4736]{2,1,0:T(2,128)(2,1)S(1)} %all-to-all-done.refs_1_, f32[2,128]{1,0:T(2,128)S(1)} %get-tuple-element.27.refs_2_, f32[2,128]{1,0:T(2,128)S(1)} %get-tuple-element.28.refs_3_, ...), custom_call_target="tpu_custom_call" | custom-call | flops 33554432 | bytes 2097152 | tf_op jit(solution)/shard_map/pallas_call | solution.py:326
  29.4 3.3 %all-to-all-start.1 = ((bf16[8,2,640]{2,1,0:T(2,128)(2,1)}), bf16[8,2,640]{2,1,0:T(2,128)(2,1)S(1)}, u32[]{:S(2)}, u32[]{:S(2)}) async-start(bf16[8,2,640]{2,1,0:T(2,128)(2,1)} %get-tuple-element.9), calls=%async_computation.1 | async-start | bytes 40960 | tf_op jit(solution)/shard_map/all_to_all | solution.py:447
  32.7 6.5 %all-to-all-done.1.x = bf16[8,2,640]{2,1,0:T(2,128)(2,1)S(1)} async-done(((bf16[8,2,640]{2,1,0:T(2,128)(2,1)}), bf16[8,2,640]{2,1,0:T(2,128)(2,1)S(1)}, u32[]{:S(2)}, u32[]{:S(2)}) %all-to-all-start.1) | async-done | bytes 20512 | tf_op jit(solution)/shard_map/all_to_all | solution.py:447
  39.2 0.0 collective-permute-done.1.other_ref
  39.2 0.0 copy-start.1
  39.2 5.3 %shard_map.125 = bf16[8,2,8192]{2,1,0:T(2,128)(2,1)} custom-call(s32[1]{0:T(128)} %bitcast.mine, s32[1]{0:T(128)S(6)} %copy.13.per_block, s32[128]{0:T(128)S(1)} %copy-done.2, s32[1]{0:T(128)} %bitcast.1.side, bf16[8,2,640]{2,1,0:T(2,128)(2,1)S(1)} %all-to-all-done.1.x, bf16[512,8192]{1,0:T(8,128)(2,1)} %wo.3, bf16[64,16,1024]{2,1,0:T(8,128)(2,1)} %here_ref.5, ...), custom_call_target="tpu_custom_call" | custom-call | flops 134217728 | bytes 8388608 | tf_op jit(solution)/shard_map/pallas_call | solution.py:379
  44.5 3.4 %all-to-all-start.2 = ((bf16[8,2,8192]{2,1,0:T(2,128)(2,1)}), bf16[8,2,8192]{2,1,0:T(2,128)(2,1)S(1)}, u32[]{:S(2)}, u32[]{:S(2)}) async-start(bf16[8,2,8192]{2,1,0:T(2,128)(2,1)} %shard_map.125), calls=%async_computation.2 | async-start | bytes 524288 | tf_op jit(solution)/shard_map/all_to_all | solution.py:447
  47.9 0.9 constant_dynamic-slice_fusion.h
  48.9 7.2 %all-to-all-done.2.t = bf16[8,2,8192]{2,1,0:T(2,128)(2,1)S(1)} async-done(((bf16[8,2,8192]{2,1,0:T(2,128)(2,1)}), bf16[8,2,8192]{2,1,0:T(2,128)(2,1)S(1)}, u32[]{:S(2)}, u32[]{:S(2)}) %all-to-all-start.2) | async-done | bytes 262176 | tf_op jit(solution)/shard_map/all_to_all | solution.py:447
  56.1 0.0 copy-done.1
  56.1 0.3 shard_map.126
  56.4 10.9 %all_to_all.40.refs_0_ = bf16[8,2,8192]{2,1,0:T(2,128)(2,1)S(1)} all-to-all(bf16[8,2,8192]{2,1,0:T(2,128)(2,1)S(1)} %get-tuple-element.10), channel_id=1, replica_groups=mesh['parts'=2,'req'=2,'tp'=8] {'tp'}, dimensions={0} | all-to-all | bytes 524288 | tf_op jit(solution)/shard_map/all_to_all | solution.py:447
  67.2 5.0 %shard_map.127 = bf16[8,2,640]{2,1,0:T(2,128)(2,1)} custom-call(bf16[8,2,8192]{2,1,0:T(2,128)(2,1)S(1)} %all_to_all.40.refs_0_, bf16[8192,512]{1,0:T(8,128)(2,1)} %refs_1_.1, bf16[8192,128]{1,0:T(8,128)(2,1)} %refs_2_.3), custom_call_target="tpu_custom_call" | custom-call | flops 167772160 | bytes 10485760 | tf_op jit(solution)/shard_map/pallas_call | solution.py:141
  72.2 3.4 %all-to-all-start.4 = ((bf16[8,2,640]{2,1,0:T(2,128)(2,1)}), bf16[8,2,640]{2,1,0:T(2,128)(2,1)S(1)}, u32[]{:S(2)}, u32[]{:S(2)}) async-start(bf16[8,2,640]{2,1,0:T(2,128)(2,1)} %shard_map.127), calls=%async_computation.4 | async-start | bytes 40960 | tf_op jit(solution)/shard_map/all_to_all | solution.py:447
  75.6 0.1 pad_maximum_fusion.3
  75.7 6.5 %all-to-all-done.4.refs_1_ = bf16[8,2,640]{2,1,0:T(2,128)(2,1)S(1)} async-done(((bf16[8,2,640]{2,1,0:T(2,128)(2,1)}), bf16[8,2,640]{2,1,0:T(2,128)(2,1)S(1)}, u32[]{:S(2)}, u32[]{:S(2)}) %all-to-all-start.4) | async-done | bytes 20512 | tf_op jit(solution)/shard_map/all_to_all | solution.py:447
  82.1 3.5 %shard_map.128 = (bf16[8,2,640]{2,1,0:T(2,128)(2,1)S(1)}, bf16[2,1024]{1,0:T(2,128)(2,1)S(1)}) custom-call(s32[2]{0:T(128)S(1)} %copy-done.3, bf16[8,2,640]{2,1,0:T(2,128)(2,1)S(1)} %all-to-all-done.4.refs_1_, bf16[2,1024]{1,0:T(2,128)(2,1)S(1)} %get-tuple-element.11.refs_2_, f32[2,128]{1,0:T(2,128)S(1)} %get-tuple-element.29.refs_3_, ...), custom_call_target="tpu_custom_call" | custom-call | flops 33554432 | bytes 2097152 | tf_op jit(solution)/shard_map/pallas_call | solution.py:326
  85.6 9.0 %all_to_all.41.x = bf16[8,2,640]{2,1,0:T(2,128)(2,1)S(1)} all-to-all(bf16[8,2,640]{2,1,0:T(2,128)(2,1)S(1)} %get-tuple-element.13), channel_id=1, replica_groups=mesh['parts'=2,'req'=2,'tp'=8] {'tp'}, dimensions={0} | all-to-all | bytes 40960 | tf_op jit(solution)/shard_map/all_to_all | solution.py:447
  94.6 4.5 %shard_map.129 = bf16[8,2,8192]{2,1,0:T(2,128)(2,1)S(1)} custom-call(s32[1]{0:T(128)} %bitcast.mine, s32[1]{0:T(128)S(6)} %copy.13.per_block, s32[128]{0:T(128)S(1)} %copy-done.2, s32[1]{0:T(128)} %bitcast.1.side, bf16[8,2,640]{2,1,0:T(2,128)(2,1)S(1)} %all_to_all.41.x, bf16[512,8192]{1,0:T(8,128)(2,1)} %wo.3, bf16[64,16,1024]{2,1,0:T(8,128)(2,1)} %here_ref.5, ...), custom_call_target="tpu_custom_call" | custom-call | flops 134217728 | bytes 8388608 | tf_op jit(solution)/shard_map/pallas_call | solution.py:379
  99.1 10.6 %all_to_all.42.t = bf16[8,2,8192]{2,1,0:T(2,128)(2,1)S(1)} all-to-all(bf16[8,2,8192]{2,1,0:T(2,128)(2,1)S(1)} %shard_map.129), channel_id=1, replica_groups=mesh['parts'=2,'req'=2,'tp'=8] {'tp'}, dimensions={0} | all-to-all | bytes 524288 | tf_op jit(solution)/shard_map/all_to_all | solution.py:447
  109.8 0.8 shard_map.130
  110.5 3.4 %all-to-all-start.7 = ((bf16[8,2,8192]{2,1,0:T(2,128)(2,1)}), bf16[8,2,8192]{2,1,0:T(2,128)(2,1)S(1)}, u32[]{:S(2)}, u32[]{:S(2)}) async-start(bf16[8,2,8192]{2,1,0:T(2,128)(2,1)} %shard_map.130), calls=%async_computation.7 | async-start | bytes 524288 | tf_op jit(solution)/shard_map/all_to_all | solution.py:447
  114.0 0.6 pad_maximum_fusion
  114.6 7.5 %all-to-all-done.7 = bf16[8,2,8192]{2,1,0:T(2,128)(2,1)S(1)} async-done(((bf16[8,2,8192]{2,1,0:T(2,128)(2,1)}), bf16[8,2,8192]{2,1,0:T(2,128)(2,1)S(1)}, u32[]{:S(2)}, u32[]{:S(2)}) %all-to-all-start.7) | async-done | bytes 262176 | tf_op jit(solution)/shard_map/all_to_all | solution.py:447
  122.1 0.8 reshape.28
  (2 shorter events, 0.0 us)
Async XLA Ops:
  0.6 38.6 %collective-permute-start.1 = (bf16[64,16,1024]{2,1,0:T(8,128)(2,1)}, bf16[64,16,1024]{2,1,0:T(8,128)(2,1)}, u32[]{:S(2)}, u32[]{:S(2)}) collective-permute-start(bf16[64,16,1024]{2,1,0:T(8,128)(2,1)} %here_ref.5), channel_id=1, source_target_pairs={{0,8},{8,0},{1,9},{9,1},{2,10},{10,2},{3,11},{11,3},{4,12},{12,4},... | collective-permute-start | bytes 6291464 | tf_op jit(solution)/shard_map/ppermute | solution.py:479
  1.1 7.3 %collective-permute-start = (bf16[64,16,512]{2,1,0:T(8,128)(2,1)}, bf16[64,16,512]{2,1,0:T(8,128)(2,1)}, u32[]{:S(2)}, u32[]{:S(2)}) collective-permute-start(bf16[64,16,512]{2,1,0:T(8,128)(2,1)} %here_ref.3), channel_id=1, source_target_pairs={{0,8},{8,0},{1,9},{9,1},{2,10},{10,2},{3,11},{11,3},{4,12},{12,4},... | collective-permute-start | bytes 3145736 | tf_op jit(solution)/shard_map/ppermute | solution.py:478
  1.9 6.6 %copy-start.3 = (s32[2]{0:T(128)S(1)}, s32[2]{0:T(128)}, u32[]{:S(2)}) copy-start(s32[2]{0:T(128)} %refs_0_.5) | copy-start | bytes 28
  1.9 6.6 %copy-start.2 = (s32[128]{0:T(128)S(1)}, s32[128]{0:T(128)}, u32[]{:S(2)}) copy-start(s32[128]{0:T(128)} %slots.5) | copy-start | bytes 1540
  8.4 16.9 %copy-start = (bf16[2,512,1024]{2,1,0:T(8,128)(2,1)S(1)}, bf16[2,512,1024]{2,1,0:T(8,128)(2,1)}, u32[]{:S(2)}) copy-start(bf16[2,512,1024]{2,1,0:T(8,128)(2,1)} %refs_5_.1) | copy-start | bytes 6291460
  10.5 14.8 %all-to-all-start = ((bf16[8,2,4736]{2,1,0:T(2,128)(2,1)}), bf16[8,2,4736]{2,1,0:T(2,128)(2,1)S(1)}, u32[]{:S(2)}, u32[]{:S(2)}) async-start(bf16[8,2,4736]{2,1,0:T(2,128)(2,1)} %shard_map.123), calls=%async_computation | async-start | bytes 303104 | tf_op jit(solution)/shard_map/all_to_all | solution.py:447
  29.4 9.9 %all-to-all-start.1 = ((bf16[8,2,640]{2,1,0:T(2,128)(2,1)}), bf16[8,2,640]{2,1,0:T(2,128)(2,1)S(1)}, u32[]{:S(2)}, u32[]{:S(2)}) async-start(bf16[8,2,640]{2,1,0:T(2,128)(2,1)} %get-tuple-element.9), calls=%async_computation.1 | async-start | bytes 40960 | tf_op jit(solution)/shard_map/all_to_all | solution.py:447
  39.2 16.9 %copy-start.1 = (bf16[8192]{0:T(1024)(128)(2,1)S(1)}, bf16[8192]{0:T(1024)(128)(2,1)}, u32[]{:S(2)}) copy-start(bf16[8192]{0:T(1024)(128)(2,1)} %param.12) | copy-start | bytes 49156
  44.5 11.6 %all-to-all-start.2 = ((bf16[8,2,8192]{2,1,0:T(2,128)(2,1)}), bf16[8,2,8192]{2,1,0:T(2,128)(2,1)S(1)}, u32[]{:S(2)}, u32[]{:S(2)}) async-start(bf16[8,2,8192]{2,1,0:T(2,128)(2,1)} %shard_map.125), calls=%async_computation.2 | async-start | bytes 524288 | tf_op jit(solution)/shard_map/all_to_all | solution.py:447
  72.2 9.9 %all-to-all-start.4 = ((bf16[8,2,640]{2,1,0:T(2,128)(2,1)}), bf16[8,2,640]{2,1,0:T(2,128)(2,1)S(1)}, u32[]{:S(2)}, u32[]{:S(2)}) async-start(bf16[8,2,640]{2,1,0:T(2,128)(2,1)} %shard_map.127), calls=%async_computation.4 | async-start | bytes 40960 | tf_op jit(solution)/shard_map/all_to_all | solution.py:447
  110.5 11.6 %all-to-all-start.7 = ((bf16[8,2,8192]{2,1,0:T(2,128)(2,1)}), bf16[8,2,8192]{2,1,0:T(2,128)(2,1)S(1)}, u32[]{:S(2)}, u32[]{:S(2)}) async-start(bf16[8,2,8192]{2,1,0:T(2,128)(2,1)} %shard_map.130), calls=%async_computation.7 | async-start | bytes 524288 | tf_op jit(solution)/shard_map/all_to_all | solution.py:447

commit v4 on v3

--- a/solution.py
+++ b/solution.py
@@ -58,21 +58,20 @@
     return copies
 
 
-def project(weights, chunk_of, rows, step, copies):
+def project(weights, chunk_of, rows, step, copies=None):
     depth = weights[0].shape[0]
-
-    def loop(i, sums):
-        at = pl.multiple_of(i * step, step)
-        for copy in copies(i):
-            copy.wait()
+    sums = [jnp.zeros((rows, w.shape[1]), f32) for w in weights]
+    for i in range(depth // step):
+        at = i * step
+        if copies is not None:
+            for copy in copies(i):
+                copy.wait()
         part = chunk_of(at, step)
-        return tuple(
-            total + jnp.dot(part, w[pl.ds(at, step), :], preferred_element_type=f32)
+        sums = [
+            total + jnp.dot(part, w[at : at + step, :], preferred_element_type=f32)
             for total, w in zip(sums, weights)
-        )
-
-    zero = tuple(jnp.zeros((rows, w.shape[1]), f32) for w in weights)
-    return lax.fori_loop(0, depth // step, loop, zero)
+        ]
+    return sums
 
 
 def store_shares(out, query, pair):
@@ -84,73 +83,86 @@
         out[j, :, width:] = pair[lines].astype(bf16)
 
 
-def projection(source, weights, own, scale=None):
-    width = weights[0].shape[0]
-    shares = lax.axis_size("tp")
-    rows = shares * own
+def cost(flops, data_bytes):
+    return pl.CostEstimate(flops=flops, bytes_accessed=data_bytes, transcendentals=0)
+
+
+def first_projection(source, scale, weights, own):
+    rows, width = source.shape
+    shares = rows // own
     message = sum(w.shape[1] for w in weights)
     step = 1024
     parts = width // step
-    first = scale is not None
-
-    def body(*refs):
-        if first:
-            source_ref, s, wq, wp, out, kept_q, kept_p, sems, x, gains, normed, pre = refs
-            loads = [
-                pltpu.make_async_copy(source_ref, x, pre.at[0]),
-                pltpu.make_async_copy(s, gains, pre.at[1]),
-            ]
-            for load in loads:
-                load.start()
-        else:
-            x, wq, wp, out, kept_q, kept_p, sems = refs
+
+    def body(mine, source_ref, s, wq, wp, out, held, kept_q, kept_p, sems, x, gains, wide, normed, pre):
+        loads = [
+            pltpu.make_async_copy(source_ref, x, pre.at[0]),
+            pltpu.make_async_copy(s, gains, pre.at[1]),
+        ]
+        for load in loads:
+            load.start()
         copies = streamed((wq, wp), (kept_q, kept_p), sems, step, 0)
         for i in range(parts):
             for copy in copies(i):
                 copy.start()
-        if first:
-            for load in loads:
-                load.wait()
-            wide = x[...].astype(f32)
-            ratio = lax.rsqrt(jnp.mean(wide * wide, axis=-1, keepdims=True) + norm_epsilon)
-            gain = gains[...].astype(f32)
-            for c in range(width // HEAD_SIZE):
-                columns = slice(c * HEAD_SIZE, (c + 1) * HEAD_SIZE)
-                normed[:, columns] = (
-                    x[:, columns].astype(f32) * ratio * gain[c : c + 1, :]
-                ).astype(bf16)
-            chunk_of = lambda at, n: normed[:, pl.ds(at, n)]
-        else:
-            chunk_of = lambda at, n: rows_of(x, at, n)
-        sums = project((kept_q, kept_p), chunk_of, rows, step, copies)
+        for load in loads:
+            load.wait()
+        wide[...] = x[...].astype(f32)
+        lines = wide[:own, :]
+        for j in range(1, shares):
+            lines = jnp.where(mine[0] == j, wide[j * own : (j + 1) * own, :], lines)
+        held[...] = lines.astype(bf16)
+        value = wide[...]
+        ratio = lax.rsqrt(jnp.mean(value * value, axis=-1, keepdims=True) + norm_epsilon)
+        gain = gains[...].astype(f32)
+        for c in range(width // HEAD_SIZE):
+            columns = slice(c * HEAD_SIZE, (c + 1) * HEAD_SIZE)
+            normed[:, columns] = (wide[:, columns] * ratio * gain[c : c + 1, :]).astype(bf16)
+        sums = project(
+            (kept_q, kept_p), lambda at, n: normed[:, at : at + n], rows, step, copies
+        )
         store_shares(out, *sums)
 
-    scratch = [pltpu.VMEM(w.shape, bf16) for w in weights]
-    scratch.append(pltpu.SemaphoreType.DMA((2, parts)))
-    operands = [source, *map(far, weights)]
-    specs = [whole(), whole(pltpu.HBM), whole(pltpu.HBM)]
-    if first:
-        operands[:1] = [far(source), far(scale)]
-        specs[:1] = [whole(pltpu.HBM)] * 2
-        scratch += [
+    return pl.pallas_call(
+        body,
+        out_shape=(
+            jax.ShapeDtypeStruct((shares, own, message), bf16),
+            jax.ShapeDtypeStruct((own, width), bf16),
+        ),
+        in_specs=[whole(pltpu.SMEM)] + [whole(pltpu.HBM)] * 4,
+        out_specs=(whole(), whole()),
+        scratch_shapes=[pltpu.VMEM(w.shape, bf16) for w in weights]
+        + [
+            pltpu.SemaphoreType.DMA((2, parts)),
             pltpu.VMEM(source.shape, bf16),
             pltpu.VMEM(scale.shape, bf16),
+            pltpu.VMEM(source.shape, f32),
             pltpu.VMEM(source.shape, bf16),
             pltpu.SemaphoreType.DMA((2,)),
-        ]
-    return pl.pallas_call(
+        ],
+        compiler_params=pltpu.CompilerParams(vmem_limit_bytes=24 * MIB),
+        cost_estimate=cost(2 * rows * width * message, 2 * width * message),
+    )(own_index("tp"), far(source), far(scale), *map(far, weights))
+
+
+def next_projection(normed, weights):
+    shares, own, width = normed.shape
+    message = sum(w.shape[1] for w in weights)
+
+    def body(x, wq, wp, out):
+        store_shares(out, *project((wq, wp), lambda at, n: rows_of(x, at, n), shares * own, 1024))
+
+    return call(
         body,
-        out_shape=jax.ShapeDtypeStruct((shares, own, message), bf16),
-        in_specs=specs,
-        out_specs=whole(),
-        scratch_shapes=scratch,
-        compiler_params=pltpu.CompilerParams(vmem_limit_bytes=24 * MIB),
-        cost_estimate=pl.CostEstimate(
-            flops=2 * rows * width * message,
-            bytes_accessed=2 * width * message,
-            transcendentals=0,
-        ),
-    )(*operands)
+        jax.ShapeDtypeStruct((shares, own, message), bf16),
+        [whole()] * 3,
+        2 * shares * own * width * message,
+        2 * width * message,
+    )(normed, *weights)
+
+
+def own_index(axis):
+    return lax.axis_index(axis).astype(jnp.int32).reshape(1)
 
 
 def fetch(block, per_block, slots, side, here, other, target, sem):
@@ -170,15 +182,18 @@
     return pltpu.make_async_copy(here.at[0], target.at[block], sem.at[block])
 
 
-def add_down(message, adapters, here, other, blocks):
+def add_adapters(message, adapters, stores, others, blocks):
     shares, own, width = message.shape
-    rank, columns = here.shape[1:]
+    _, rank, columns = stores[0].shape
     lead = rank // own * columns
 
-    def body(per_block, slots, side, m, here_ref, other_ref, out, piece, sem):
+    def body(per_block, slots, side, m, down, up, other_down, other_up, out, ups, piece, sem):
         waits = [
-            fetch(b, per_block, slots, side, here_ref, other_ref, piece, sem)
+            fetch(b, per_block, slots, side, here, other, target, sem.at[n])
             for b in range(blocks)
+            for n, (here, other, target) in enumerate(
+                ((down, other_down, piece), (up, other_up, ups))
+            )
         ]
         for j in range(shares):
             out[j, :, lead:] = m[j]
@@ -195,18 +210,21 @@
     smem = whole(pltpu.SMEM)
     return pl.pallas_call(
         body,
-        out_shape=jax.ShapeDtypeStruct((shares, own, lead + width), bf16),
-        in_specs=[smem, smem, smem, whole(), whole(pltpu.HBM), whole(pltpu.HBM)],
-        out_specs=whole(),
+        out_shape=(
+            jax.ShapeDtypeStruct((shares, own, lead + width), bf16),
+            jax.ShapeDtypeStruct((blocks,) + stores[1].shape[1:], bf16),
+        ),
+        in_specs=[smem, smem, smem, whole()] + [whole(pltpu.HBM)] * 4,
+        out_specs=(whole(), whole()),
         scratch_shapes=[
             pltpu.VMEM((blocks, rank, columns), bf16),
-            pltpu.SemaphoreType.DMA((blocks,)),
+            pltpu.SemaphoreType.DMA((2, blocks)),
         ],
         compiler_params=pltpu.CompilerParams(vmem_limit_bytes=16 * MIB),
-    )(*adapters, message, far(here), far(other))
-
-
-def attend(arrived, pairs, older, angles, lengths, cache, down, step, lead, rank):
+    )(*adapters, message, *map(far, stores), *map(far, others))
+
+
+def attend(arrived, pairs, older, lengths, cache, down, step, lead, rank):
     shares, own, message = arrived.shape
     context, width = cache.shape[1:]
     half = width // 2
@@ -220,24 +238,29 @@
         lens, x = refs.pop(0), refs.pop(0)
         pair_ref = None if pair_inside else refs.pop(0)
         old = refs.pop(0) if step else None
-        cos_ref, sin_ref, kv = refs[:3]
+        kv = refs.pop(0)
         if step:
-            down_ref, out, new = refs[3:]
+            down_ref, out, new = refs
         else:
-            out, new, down_ref = refs[3:]
+            out, new, down_ref = refs
             for j in range(shares):
                 lines = [
                     x[j, :, m * query_width : (m + 1) * query_width].astype(f32)
                     for m in range(rank // own)
                 ]
                 down_ref[j] = jnp.concatenate(lines, axis=0).astype(bf16)
+        half_head = HEAD_SIZE // 2
+        lane = lax.broadcasted_iota(jnp.int32, (1, HEAD_SIZE), 1)
+        entry = jnp.where(lane < half_head, lane, lane - half_head).astype(f32)
+        frequency = jnp.exp(entry * f32(-2.0 / HEAD_SIZE * math.log(rope_base)))
         place = lax.broadcasted_iota(jnp.int32, (groups, context), 1)
         rows = [x[j, :, lead:].astype(f32) for j in range(shares)]
         outputs = []
         fresh = []
         for r in range(own):
-            cosine = cos_ref[r : r + 1, :]
-            sine = sin_ref[r : r + 1, :]
+            angle = (lens[r] + step).astype(f32) * frequency
+            cosine = jnp.cos(angle)
+            sine = jnp.where(lane < half_head, -jnp.sin(angle), jnp.sin(angle))
 
             def turn(v):
                 return v * cosine + pltpu.roll(v, HEAD_SIZE // 2, 1) * sine
@@ -291,7 +314,12 @@
                     result = result + (e / total).astype(bf16).astype(f32) * v
                 heads.append(result)
             outputs.append(heads)
-        new[...] = jnp.concatenate(fresh, axis=0).astype(bf16)
+        fresh = jnp.concatenate(fresh, axis=0).astype(bf16)
+        if step < STEPS - 1:
+            new[...] = fresh
+        else:
+            new[0] = old[...]
+            new[1] = fresh
         low = jnp.zeros((own, rank), f32)
         for j in range(shares):
             lines = []
@@ -315,11 +343,11 @@
     for extra in ([] if pair_inside else [pairs]) + ([older] if step else []):
         operands.append(extra)
         specs.append(whole())
-    operands += [angles[0], angles[1], cache] + ([down] if step else [])
-    specs += [whole()] * (4 if step else 3)
+    operands += [cache] + ([down] if step else [])
+    specs += [whole()] * (2 if step else 1)
     outs = [
         jax.ShapeDtypeStruct((shares, own, query_width + HEAD_SIZE), bf16),
-        jax.ShapeDtypeStruct((own, width), bf16),
+        jax.ShapeDtypeStruct((own, width) if step < STEPS - 1 else (STEPS, own, width), bf16),
     ]
     if not step:
         outs.append(jax.ShapeDtypeStruct((shares, rank, query_width), bf16))
@@ -337,71 +365,40 @@
     )(*operands)
 
 
-def output_terms(arrived, output_weight, adapters, here, other, blocks):
+def output_terms(arrived, output_weight, up):
     shares, own, _ = arrived.shape
     query_width, width = output_weight.shape
-    rank, share_width = here.shape[1:]
+    blocks, rank, share_width = up.shape
     rows = shares * own
     step = 1024
-    parts = width // step
-
-    def body(mine, per_block, slots, side, x, wo, here_ref, other_ref, *refs):
-        out, total, kept, up, sem, sems = refs
-        copies = streamed((wo,), (kept,), sems, step, 1)
-        for i in range(parts):
-            copies(i)[0].start()
-        waits = [
-            fetch(b, per_block, slots, side, here_ref, other_ref, up, sem) for b in range(blocks)
-        ]
+
+    def body(mine, x, wo, up_ref, out, added):
         heads = rows_of(x, 0, query_width)
         low = rows_of(x, query_width, HEAD_SIZE)[:, :rank]
-
-        def loop(i, carry):
-            at = pl.multiple_of(i * step, step)
-            copies(i)[0].wait()
-            total[:, pl.ds(at, step)] = jnp.dot(
-                heads, kept[:, pl.ds(at, step)], preferred_element_type=f32
-            )
-            return carry
-
-        lax.fori_loop(0, parts, loop, 0)
+        added[...] = jnp.zeros_like(added)
         start = pl.multiple_of(mine[0] * share_width, share_width)
         for b in range(blocks):
-            waits[b].wait()
             lines = slice(b * BLOCK, (b + 1) * BLOCK)
-            total[lines, pl.ds(start, share_width)] += jnp.dot(
-                low[lines], up[b], preferred_element_type=f32
+            added[lines, pl.ds(start, share_width)] = jnp.dot(
+                low[lines], up_ref[b], preferred_element_type=f32
             )
-        for j in range(shares):
-            out[j] = total[j * own : (j + 1) * own, :].astype(out.dtype)
-
-    smem, hbm = whole(pltpu.SMEM), whole(pltpu.HBM)
+        for i in range(width // step):
+            columns = slice(i * step, (i + 1) * step)
+            total = added[:, columns] + jnp.dot(
+                heads, wo[:, columns], preferred_element_type=f32
+            )
+            for j in range(shares):
+                out[j, :, columns] = total[j * own : (j + 1) * own, :].astype(out.dtype)
+
     return pl.pallas_call(
         body,
         out_shape=jax.ShapeDtypeStruct((shares, own, width), term_type),
-        in_specs=[smem] * 4 + [whole(), hbm, hbm, hbm],
+        in_specs=[whole(pltpu.SMEM)] + [whole()] * 3,
         out_specs=whole(),
-        scratch_shapes=[
-            pltpu.VMEM((rows, width), f32),
-            pltpu.VMEM(output_weight.shape, bf16),
-            pltpu.VMEM((blocks, rank, share_width), bf16),
-            pltpu.SemaphoreType.DMA((blocks,)),
-            pltpu.SemaphoreType.DMA((1, parts)),
-        ],
-        compiler_params=pltpu.CompilerParams(vmem_limit_bytes=24 * MIB),
-        cost_estimate=pl.CostEstimate(
-            flops=2 * rows * width * query_width,
-            bytes_accessed=2 * width * query_width,
-            transcendentals=0,
-        ),
-    )(
-        lax.axis_index("tp").astype(jnp.int32).reshape(1),
-        *adapters,
-        arrived,
-        far(output_weight),
-        far(here),
-        far(other),
-    )
+        scratch_shapes=[pltpu.VMEM((rows, width), f32)],
+        compiler_params=pltpu.CompilerParams(vmem_limit_bytes=16 * MIB),
+        cost_estimate=cost(2 * rows * width * query_width, 2 * width * query_width),
+    )(own_index("tp"), arrived, output_weight, up)
 
 
 def close_step(terms, hidden, scale):
@@ -460,8 +457,6 @@
     adapter_down_projection,
     adapter_up_projection,
 ):
-    tp_count = lax.axis_size("tp")
-    tp_index = lax.axis_index("tp")
     rows_req = input_hidden_rows.shape[0]
     own = cache.shape[0]
     blocks = rows_req // BLOCK
@@ -472,58 +467,34 @@
     adapters = (
         adapter_per_block,
         adapter_storage_slot,
-        lax.axis_index("req").astype(jnp.int32).reshape(1),
+        own_index("req"),
     )
     cores = [(0, 1), (1, 0)]
-    other_down = lax.ppermute(adapter_down_projection, "req", cores)
-    other_up = lax.ppermute(adapter_up_projection, "req", cores)
+    stores = (adapter_down_projection, adapter_up_projection)
+    others = [lax.ppermute(store, "req", cores) for store in stores]
     lead = rank // own * query_width
-    half_head = HEAD_SIZE // 2
-    frequency = rope_base ** (-(jnp.arange(half_head, dtype=f32) * 2.0 / HEAD_SIZE))
-    hidden = lax.dynamic_slice_in_dim(input_hidden_rows, tp_index * own, own, 0)
-    stored = []
     weights = (query_weight, key_value_weight)
-    message = projection(input_hidden_rows, weights, own, scale)
-    message = add_down(message, adapters, adapter_down_projection, other_down, blocks)
-    down = None
+    message, hidden = first_projection(input_hidden_rows, scale, weights, own)
+    message, up = add_adapters(message, adapters, stores, others, blocks)
+    down = fresh = None
     for step in range(STEPS):
-        angle = (lengths + step).astype(f32)[:, None] * frequency[None, :]
-        cosine, sine = jnp.cos(angle), jnp.sin(angle)
-        angles = (
-            jnp.concatenate([cosine, cosine], axis=1),
-            jnp.concatenate([-sine, sine], axis=1),
-        )
         arrived = exchange(message)
         start = 0 if step else lead
         pairs = None
         if key_value_weight.shape[1] != HEAD_SIZE:
             pairs = arrived[:, :, start + query_width :].transpose(1, 0, 2).reshape(own, -1)
         attended, fresh, *first = attend(
-            arrived,
-            pairs,
-            stored[-1] if step else None,
-            angles,
-            lengths,
-            cache,
-            down,
-            step,
-            start,
-            rank,
+            arrived, pairs, fresh, lengths, cache, down, step, start, rank
         )
-        stored.append(fresh)
         if not step:
             (down,) = first
-        terms = exchange(
-            output_terms(
-                exchange(attended), output_weight, adapters, adapter_up_projection, other_up, blocks
-            )
-        )
+        terms = exchange(output_terms(exchange(attended), output_weight, up))
         if step < STEPS - 1:
             spread, hidden = close_step(terms, hidden, scale)
-            message = projection(exchange(spread), weights, own)
+            message = next_projection(exchange(spread), weights)
         else:
             (spread,) = close_step(terms, hidden, None)
-    return (exchange(spread).reshape(rows_req, width), jnp.stack(stored, axis=0))
+    return (exchange(spread).reshape(rows_req, width), fresh)
 
 
 def solution(mesh):

time: 124 us -> 111 us (0.90)
  blocking collectives: 30.5 us -> 85.6 us
  waiting for transfers between devices: 35.1 us -> 0.01 us
  starting transfers between devices: 21.4 us -> 0.6 us
  Pallas kernels: 31.8 us -> 20.6 us
    all_to_all x3 -> x8, blocking collectives: 30.5 us -> 85.6 us  [exchange(): return lax.all_to_all(chunks, 'tp', split_axis=0, concat_axis=0, tiled=True)]
    all_to_all x5 -> x0, waiting for transfers between devices: 35.1 us -> none  [exchange(): return lax.all_to_all(chunks, 'tp', split_axis=0, concat_axis=0, tiled=True)]
    all_to_all x5 -> x0, starting transfers between devices: 20.8 us -> none  [exchange(): return lax.all_to_all(chunks, 'tp', split_axis=0, concat_axis=0, tiled=True)]
    pallas_call x2, Pallas kernels: 9.8 us -> 2.48 us  [output_terms(): pl.pallas_call(body, out_shape=jax.ShapeDtypeStruct((shares, own, width),...]
    pallas_call x3, Pallas kernels: 13.5 us -> 10.4 us  [the longest x1 6.78 us: first_projection(): pl.pallas_call(body, out_shape=(jax.ShapeDtypeStruct((shares, own, messag...]
    unnamed x8 -> x20, local copies, waits for them, and re-layouts: 0.02 us -> 1.65 us
  transfers between devices with their start and end apart: 7 -> 2, of which waited for: 5 -> 0; matrix products, arithmetic and copies ran while one was open for 2% -> 0% of each run, Pallas kernels for 10% -> 6%
where the time goes in v4:
time: 111 us
  blocking collectives  85.6 us (77%)
  Pallas kernels  20.6 us (19%)
  local copies, waits for them, and re-layouts  2.45 us (2%)
  between operations  1.4 us (1%)
    all_to_all x8, blocking collectives, exchange(): return lax.all_to_all(chunks, 'tp', split_axis=0, concat_axis=0, tiled=True)  85.6 us
    pallas_call x2, Pallas kernels, attend(): pl.pallas_call(body, out_shape=tuple(outs), in_specs=specs, out_specs=(wh...  7.37 us
    pallas_call x1, Pallas kernels, first_projection(): pl.pallas_call(body, out_shape=(jax.ShapeDtypeStruct((shares, own, messag...  6.78 us
    pallas_call x2, Pallas kernels, output_terms(): pl.pallas_call(body, out_shape=jax.ShapeDtypeStruct((shares, own, width),...  2.48 us
  transfers between devices with their start and end apart: 2, of which 0 were waited for; matrix products, arithmetic and copies ran while one was open for 0% of the time, Pallas kernels for 6%

profile of v4, /device:TPU:0, one launch (start us, length us, event | category | flops | bytes accessed | tf_op | source)
XLA Modules:
  0.0 110.7 jit_solution(2066154038779531471)
XLA Ops:
  0.6 0.5 collective-permute-start.1
  1.1 0.1 collective-permute-start
  1.9 0.0 copy-start.5
  1.9 0.0 copy-start.1
  1.9 0.0 copy-start.4
  1.9 6.8 %shard_map.122 = (bf16[8,2,640]{2,1,0:T(2,128)(2,1)S(1)}, bf16[2,8192]{1,0:T(2,128)(2,1)S(1)}) custom-call(s32[1]{0:T(128)} %bitcast.mine, bf16[16,8192]{1,0:T(8,128)(2,1)} %source_ref.1, bf16[64,128]{1,0:T(8,128)(2,1)} %bitcast.5, bf16[8192,512]{1,0:T(8,128)(2,1)} %wq.3, bf16[8192,128]{1,0:T(8,128)(2,1)} %wp.3), custom_call_target="tpu_custom_call" | custom-call | flops 167772160 | bytes 10485760 | tf_op jit(solution)/shard_map/pallas_call | solution.py:126
  8.7 0.0 collective-permute-done.other_down
  8.7 0.0 copy-start.7
  8.7 0.0 collective-permute-done.1.other_up
  8.7 0.0 copy-start.6
  8.7 0.0 copy-start
  8.7 0.9 copy-done.7
  9.7 0.7 copy-done.6
  10.4 0.0 copy-done.5
  10.4 0.0 slice-start
  10.4 2.1 %shard_map.123 = (bf16[8,2,4736]{2,1,0:T(2,128)(2,1)S(1)}, bf16[1,16,1024]{2,1,0:T(8,128)(2,1)S(1)}) custom-call(s32[1]{0:T(128)S(6)} %copy.13.per_block, s32[128]{0:T(128)S(1)} %copy-done.5, s32[1]{0:T(128)} %bitcast.1.side, bf16[8,2,640]{2,1,0:T(2,128)(2,1)S(1)} %get-tuple-element.13.m, bf16[64,16,512]{2,1,0:T(8,128)(2,1)} %down.1, ...), custom_call_target="tpu_custom_call" | custom-call | tf_op jit(solution)/shard_map/pallas_call | solution.py:211
  12.5 14.8 %all_to_all.40.refs_1_ = bf16[8,2,4736]{2,1,0:T(2,128)(2,1)S(1)} all-to-all(bf16[8,2,4736]{2,1,0:T(2,128)(2,1)S(1)} %get-tuple-element.14), channel_id=1, replica_groups=mesh['parts'=2,'req'=2,'tp'=8] {'tp'}, dimensions={0} | all-to-all | bytes 303104 | tf_op jit(solution)/shard_map/all_to_all | solution.py:444
  27.4 0.0 copy-done.1
  27.4 0.0 copy-done.4
  27.4 0.0 copy-start.3
  27.4 3.4 %shard_map.124 = (bf16[8,2,640]{2,1,0:T(2,128)(2,1)S(1)}, bf16[2,1024]{1,0:T(2,128)(2,1)S(1)}, bf16[8,16,512]{2,1,0:T(8,128)(2,1)S(1)}) custom-call(s32[2]{0:T(128)S(1)} %copy-done.4, bf16[8,2,4736]{2,1,0:T(2,128)(2,1)S(1)} %all_to_all.40.refs_1_, bf16[2,512,1024]{2,1,0:T(8,128)(2,1)S(1)} %copy-done.1), custom_call_target="tpu_custom_call" | custom-call | flops 33554432 | bytes 2097152 | tf_op jit(solution)/shard_map/pallas_call | solution.py:354
  30.8 9.3 %all_to_all.41.x = bf16[8,2,640]{2,1,0:T(2,128)(2,1)S(1)} all-to-all(bf16[8,2,640]{2,1,0:T(2,128)(2,1)S(1)} %get-tuple-element.15), channel_id=1, replica_groups=mesh['parts'=2,'req'=2,'tp'=8] {'tp'}, dimensions={0} | all-to-all | bytes 40960 | tf_op jit(solution)/shard_map/all_to_all | solution.py:444
  40.1 0.0 copy-done
  40.1 0.0 slice-start.1
  40.1 0.0 copy-start.2
  40.1 1.2 %shard_map.125 = bf16[8,2,8192]{2,1,0:T(2,128)(2,1)S(1)} custom-call(s32[1]{0:T(128)} %bitcast.mine, bf16[8,2,640]{2,1,0:T(2,128)(2,1)S(1)} %all_to_all.41.x, bf16[512,8192]{1,0:T(8,128)(2,1)S(1)} %copy-done, bf16[1,16,1024]{2,1,0:T(8,128)(2,1)S(1)} %get-tuple-element.16.up_ref), custom_call_target="tpu_custom_call" | custom-call | flops 134217728 | bytes 8388608 | tf_op jit(solution)/shard_map/pallas_call | solution.py:393
  41.3 10.8 %all_to_all.42.t = bf16[8,2,8192]{2,1,0:T(2,128)(2,1)S(1)} all-to-all(bf16[8,2,8192]{2,1,0:T(2,128)(2,1)S(1)} %shard_map.125), channel_id=1, replica_groups=mesh['parts'=2,'req'=2,'tp'=8] {'tp'}, dimensions={0} | all-to-all | bytes 524288 | tf_op jit(solution)/shard_map/all_to_all | solution.py:444
  52.1 0.0 copy-done.3
  52.1 0.3 shard_map.126
  52.4 11.0 %all_to_all.43.x = bf16[8,2,8192]{2,1,0:T(2,128)(2,1)S(1)} all-to-all(bf16[8,2,8192]{2,1,0:T(2,128)(2,1)S(1)} %get-tuple-element.18), channel_id=1, replica_groups=mesh['parts'=2,'req'=2,'tp'=8] {'tp'}, dimensions={0} | all-to-all | bytes 524288 | tf_op jit(solution)/shard_map/all_to_all | solution.py:444
  63.3 0.0 slice-done
  63.3 0.0 slice-done.1
  63.3 0.0 copy-done.2
  63.4 1.5 %shard_map.127 = bf16[8,2,640]{2,1,0:T(2,128)(2,1)S(1)} custom-call(bf16[8,2,8192]{2,1,0:T(2,128)(2,1)S(1)} %all_to_all.43.x, bf16[8192,512]{1,0:T(8,128)(2,1)S(1)} %bitcast.4, bf16[8192,128]{1,0:T(8,128)(2,1)S(1)} %copy-done.2), custom_call_target="tpu_custom_call" | custom-call | flops 167772160 | bytes 10485760 | tf_op jit(solution)/shard_map/pallas_call | solution.py:155
  64.8 9.3 %all_to_all.44.refs_1_ = bf16[8,2,640]{2,1,0:T(2,128)(2,1)S(1)} all-to-all(bf16[8,2,640]{2,1,0:T(2,128)(2,1)S(1)} %shard_map.127), channel_id=1, replica_groups=mesh['parts'=2,'req'=2,'tp'=8] {'tp'}, dimensions={0} | all-to-all | bytes 40960 | tf_op jit(solution)/shard_map/all_to_all | solution.py:444
  74.1 3.9 %shard_map.128 = (bf16[8,2,640]{2,1,0:T(2,128)(2,1)S(1)}, bf16[2,2,1024]{2,1,0:T(2,128)(2,1)}) custom-call(s32[2]{0:T(128)S(1)} %copy-done.4, bf16[8,2,640]{2,1,0:T(2,128)(2,1)S(1)} %all_to_all.44.refs_1_, bf16[2,1024]{1,0:T(2,128)(2,1)S(1)} %get-tuple-element.19.refs_2_, bf16[2,512,1024]{2,1,0:T(8,128)(2,1)S(1)} %copy-done.1, ...), custom_call_target="tpu_custom_call" | custom-call | flops 33554432 | bytes 2097152 | tf_op jit(solution)/shard_map/pallas_call | solution.py:354
  78.1 9.0 %all_to_all.45.x = bf16[8,2,640]{2,1,0:T(2,128)(2,1)S(1)} all-to-all(bf16[8,2,640]{2,1,0:T(2,128)(2,1)S(1)} %get-tuple-element.21), channel_id=1, replica_groups=mesh['parts'=2,'req'=2,'tp'=8] {'tp'}, dimensions={0} | all-to-all | bytes 40960 | tf_op jit(solution)/shard_map/all_to_all | solution.py:444
  87.0 1.2 %shard_map.129 = bf16[8,2,8192]{2,1,0:T(2,128)(2,1)S(1)} custom-call(s32[1]{0:T(128)} %bitcast.mine, bf16[8,2,640]{2,1,0:T(2,128)(2,1)S(1)} %all_to_all.45.x, bf16[512,8192]{1,0:T(8,128)(2,1)S(1)} %copy-done, bf16[1,16,1024]{2,1,0:T(8,128)(2,1)S(1)} %get-tuple-element.16.up_ref), custom_call_target="tpu_custom_call" | custom-call | flops 134217728 | bytes 8388608 | tf_op jit(solution)/shard_map/pallas_call | solution.py:393
  88.3 10.7 %all_to_all.46.t = bf16[8,2,8192]{2,1,0:T(2,128)(2,1)S(1)} all-to-all(bf16[8,2,8192]{2,1,0:T(2,128)(2,1)S(1)} %shard_map.129), channel_id=1, replica_groups=mesh['parts'=2,'req'=2,'tp'=8] {'tp'}, dimensions={0} | all-to-all | bytes 524288 | tf_op jit(solution)/shard_map/all_to_all | solution.py:444
  98.9 0.1 shard_map.130
  99.0 10.8 %all_to_all.47 = bf16[8,2,8192]{2,1,0:T(2,128)(2,1)S(1)} all-to-all(bf16[8,2,8192]{2,1,0:T(2,128)(2,1)S(1)} %shard_map.130), channel_id=1, replica_groups=mesh['parts'=2,'req'=2,'tp'=8] {'tp'}, dimensions={0} | all-to-all | bytes 524288 | tf_op jit(solution)/shard_map/all_to_all | solution.py:444
  109.9 0.8 reshape.21
  (1 shorter events, 0.0 us)
Async XLA Ops:
  0.6 8.1 %collective-permute-start.1 = (bf16[64,16,1024]{2,1,0:T(8,128)(2,1)}, bf16[64,16,1024]{2,1,0:T(8,128)(2,1)S(1)}, u32[]{:S(2)}, u32[]{:S(2)}) collective-permute-start(bf16[64,16,1024]{2,1,0:T(8,128)(2,1)} %up.1), channel_id=1, source_target_pairs={{0,8},{8,0},{1,9},{9,1},{2,10},{10,2},{3,11},{11,3},{4,12},{12,4},... | collective-permute-start | bytes 6291464 | tf_op jit(solution)/shard_map/ppermute | solution.py:474
  1.1 7.5 %collective-permute-start = (bf16[64,16,512]{2,1,0:T(8,128)(2,1)}, bf16[64,16,512]{2,1,0:T(8,128)(2,1)S(1)}, u32[]{:S(2)}, u32[]{:S(2)}) collective-permute-start(bf16[64,16,512]{2,1,0:T(8,128)(2,1)} %down.1), channel_id=1, source_target_pairs={{0,8},{8,0},{1,9},{9,1},{2,10},{10,2},{3,11},{11,3},{4,12},{12,4},... | collective-permute-start | bytes 3145736 | tf_op jit(solution)/shard_map/ppermute | solution.py:474
  1.9 8.5 %copy-start.5 = (s32[128]{0:T(128)S(1)}, s32[128]{0:T(128)}, u32[]{:S(2)}) copy-start(s32[128]{0:T(128)} %slots.1) | copy-start | bytes 1540
  1.9 25.5 %copy-start.1 = (bf16[2,512,1024]{2,1,0:T(8,128)(2,1)S(1)}, bf16[2,512,1024]{2,1,0:T(8,128)(2,1)}, u32[]{:S(2)}) copy-start(bf16[2,512,1024]{2,1,0:T(8,128)(2,1)} %refs_3_.1) | copy-start | bytes 6291460
  1.9 25.5 %copy-start.4 = (s32[2]{0:T(128)S(1)}, s32[2]{0:T(128)}, u32[]{:S(2)}) copy-start(s32[2]{0:T(128)} %refs_0_.3) | copy-start | bytes 28
  8.7 1.0 copy-start.7
  8.7 1.6 %copy-start.6 = (bf16[64,16,1024]{2,1,0:T(8,128)(2,1)}, bf16[64,16,1024]{2,1,0:T(8,128)(2,1)S(1)}, u32[]{:S(2)}) copy-start(bf16[64,16,1024]{2,1,0:T(8,128)(2,1)S(1)} %collective-permute-done.1.other_up) | copy-start | bytes 6291460
  8.7 31.3 %copy-start = (bf16[512,8192]{1,0:T(8,128)(2,1)S(1)}, bf16[512,8192]{1,0:T(8,128)(2,1)}, u32[]{:S(2)}) copy-start(bf16[512,8192]{1,0:T(8,128)(2,1)} %wo.3) | copy-start | bytes 25165828
  10.4 53.0 %slice-start = ((s8[8388608]{0:T(1024)(128)(4,1)}), s8[4194304]{0:T(1024)(128)(4,1)S(1)}, s32[]{:S(2)}) async-start(s8[8388608]{0:T(1024)(128)(4,1)} %bitcast.3), calls=%async_computation.8 | async-start | bytes 8388608
  27.4 24.7 %copy-start.3 = (bf16[8192]{0:T(1024)(128)(2,1)S(1)}, bf16[8192]{0:T(1024)(128)(2,1)}, u32[]{:S(2)}) copy-start(bf16[8192]{0:T(1024)(128)(2,1)} %param.12) | copy-start | bytes 49156
  40.1 23.3 %slice-start.1 = ((s8[8388608]{0:T(1024)(128)(4,1)}), s8[4194304]{0:T(1024)(128)(4,1)S(1)}, s32[]{:S(2)}) async-start(s8[8388608]{0:T(1024)(128)(4,1)} %bitcast.3), calls=%async_computation.9 | async-start | bytes 8388608
  40.1 23.3 %copy-start.2 = (bf16[8192,128]{1,0:T(8,128)(2,1)S(1)}, bf16[8192,128]{1,0:T(8,128)(2,1)}, u32[]{:S(2)}) copy-start(bf16[8192,128]{1,0:T(8,128)(2,1)} %wp.3) | copy-start | bytes 6291460
